TPU v7x, 32 devices: a whole 2x2x4 slice. The times are simulated.
32 devices in a mesh: dp: 16 (over z, x, core), blk: 2 (over y).
Axes of the slice: x: 2, y: 2, z: 4, core: 2. Of those that a mesh axis runs over, the one named last changes fastest.
Arguments:
- tokens: bfloat16 [32, 512, 768], P('dp', 'blk'), may hold values from -6 to 6
- boxes: int32 [2, 32, 512], P(None, 'dp', 'blk'), may hold values from 0 to 1000
- lengths: int32 [32], P('dp'), may hold values from 40 to 512, as said below
- wqkv: bfloat16 [768, 2304], P('dp', 'blk'), may hold values from -0.21875 to 0.21875
- wbox: bfloat16 [768, 768], P('dp', 'blk'), may hold values from -0.375 to 0.375
- wout: bfloat16 [768, 768], P('dp', 'blk'), may hold values from -1.75 to 1.75
- wup: bfloat16 [768, 3072], P('dp', 'blk'), may hold values from -0.21875 to 0.21875
- wdown: bfloat16 [3072, 768], P('dp', 'blk'), may hold values from -0.109375 to 0.109375
- vectors: bfloat16 [9216], P(('dp', 'blk')), may hold values from -1.5 to 1.6
- cotangent: bfloat16 [32, 512, 768], P('dp', 'blk'), may hold values from -6 to 6
Outputs:
- output: bfloat16 [32, 512, 768], P('dp', 'blk')
- tokens_grad: float32 [32, 512, 768], P('dp', 'blk')
- wqkv_grad: float32 [768, 2304], P('dp', 'blk')
- wbox_grad: float32 [768, 768], P('dp', 'blk')
- wout_grad: float32 [768, 768], P('dp', 'blk')
- wup_grad: float32 [768, 3072], P('dp', 'blk')
- wdown_grad: float32 [3072, 768], P('dp', 'blk')
- vectors_grad: float32 [9216], P(('dp', 'blk'))
Inputs may be any that keep to these rules, and one draw needn't show every extreme that they name: `lengths`: in each run of 2 pages that one index of dp holds, one page, drawn from the seed, has more than 256 real tokens; one page of all, drawn from the seed, has all 512.
All inputs are finite; a program needn't handle non-finite values.
Results may differ from a plain program's by a relative error of at most 0.023.
Values may be sent and summed in bfloat16 or wider, within the bound.
A program may use at most 256 MiB of HBM per device.

v0:
```python
from functools import partial
import math

import jax
import jax.numpy as jnp
import numpy as np
from jax import lax
from jax.experimental import pallas as pl
from jax.experimental.pallas import tpu as pltpu
from jax.sharding import PartitionSpec as P

HEADS = 12
HEAD = 64
FREQ = 192
BOX_DIM = 768

EPSILON = 1e-12
MASKED = -1e30


def box_table(boxes):
    frequency = jnp.exp(jnp.arange(FREQ, dtype=jnp.float32) * (-math.log(10000.0) / FREQ))
    across = boxes[0].astype(jnp.float32)[..., None] * frequency
    upward = boxes[1].astype(jnp.float32)[..., None] * frequency
    return jnp.concatenate(
        [jnp.cos(across), jnp.sin(across), jnp.cos(upward), jnp.sin(upward)], axis=-1
    )


def rotate(coeffs, own_table):
    cos_across, sin_across, cos_upward, sin_upward = jnp.split(own_table[..., None, :], 4, axis=-1)
    sa, ca, sb, cb = jnp.split(coeffs, 4, axis=-1)
    return jnp.concatenate(
        [
            sa * sin_across + ca * cos_across,
            ca * sin_across - sa * cos_across,
            sb * sin_upward + cb * cos_upward,
            cb * sin_upward - sb * cos_upward,
        ],
        axis=-1,
    )


def unrotate(grad_rows, own_table):
    cos_across, sin_across, cos_upward, sin_upward = jnp.split(own_table[..., None, :], 4, axis=-1)
    d1a, d2a, d1b, d2b = jnp.split(grad_rows, 4, axis=-1)
    return jnp.concatenate(
        [
            d1a * sin_across - d2a * cos_across,
            d1a * cos_across + d2a * sin_across,
            d1b * sin_upward - d2b * cos_upward,
            d1b * cos_upward + d2b * sin_upward,
        ],
        axis=-1,
    )


def normalize(hidden):
    row_mean = jnp.mean(hidden, axis=-1, keepdims=True)
    centered = hidden - row_mean
    inverse = lax.rsqrt(jnp.mean(centered * centered, axis=-1, keepdims=True) + EPSILON)
    return centered * inverse, inverse


def normalize_back(grad, unit, inverse, gain):
    scaled = grad * gain
    mean_grad = jnp.mean(scaled, axis=-1, keepdims=True)
    mean_unit = jnp.mean(scaled * unit, axis=-1, keepdims=True)
    d_hidden = inverse * (scaled - mean_grad - unit * mean_unit)
    return d_hidden, jnp.sum(grad * unit, axis=0), jnp.sum(grad, axis=0)


def unpack(vector_all, model_width, hidden_units):
    cuts = [model_width] * 5 + [hidden_units] + [model_width] * 3
    pieces = []
    offset = 0
    for length_here in cuts:
        pieces.append(vector_all[offset : offset + length_here])
        offset = offset + length_here
    return pieces


def dot32(a, b):
    return jnp.dot(a, b, preferred_element_type=jnp.float32)


def gather_weight(shard):
    part = lax.all_gather(shard, "blk", axis=1, tiled=True)
    return lax.all_gather(part, "dp", axis=0, tiled=True)


def scatter_weight(grad):
    part = lax.psum_scatter(grad.astype(jnp.bfloat16), "dp", scatter_dimension=0, tiled=True)
    return lax.psum_scatter(part, "blk", scatter_dimension=1, tiled=True).astype(jnp.float32)


def general_layer(tokens, boxes, lengths, wqkv, wbox, wout, wup, wdown, vectors, cotangent):
    blocks = lax.axis_size("blk")
    pages_here = tokens.shape[0] // blocks
    model_width = tokens.shape[2]
    to_pages = partial(
        lax.all_to_all, axis_name="blk", split_axis=0, concat_axis=1, tiled=True
    )
    from_pages = partial(
        lax.all_to_all, axis_name="blk", split_axis=1, concat_axis=0, tiled=True
    )
    page_tokens = to_pages(tokens)
    page_boxes = lax.all_to_all(boxes, "blk", split_axis=1, concat_axis=2, tiled=True)
    page_lengths = lax.dynamic_slice(lengths, (lax.axis_index("blk") * pages_here,), (pages_here,))
    full_qkv = gather_weight(wqkv)
    full_box = gather_weight(wbox)
    full_out = gather_weight(wout)
    full_up = gather_weight(wup)
    full_down = gather_weight(wdown)
    full_vec = lax.all_gather(vectors, ("dp", "blk"), axis=0, tiled=True).astype(jnp.float32)
    page_cotangent = to_pages(cotangent)
    hidden_units = full_up.shape[1]
    bq, bv, bo, g1, e1, b1, b2, g2, e2 = unpack(full_vec, model_width, hidden_units)
    page_len = page_tokens.shape[1]
    score_scale = HEAD ** (-0.5)

    x = page_tokens.reshape(-1, model_width)
    projected = dot32(x, full_qkv)
    head_shape = (pages_here, page_len, HEADS, HEAD)
    q = (projected[:, :model_width] + bq).astype(jnp.bfloat16).reshape(head_shape)
    k = projected[:, model_width : 2 * model_width].astype(jnp.bfloat16).reshape(head_shape)
    v = (projected[:, 2 * model_width :] + bv).astype(jnp.bfloat16).reshape(head_shape)
    table = box_table(page_boxes)
    box_heads = full_box.reshape(HEADS, HEAD, BOX_DIM)
    coeffs = jnp.einsum("pqhd,hdc->pqhc", q, box_heads, preferred_element_type=jnp.float32)
    box_query = rotate(coeffs, table).astype(jnp.bfloat16)
    box_keys = table.astype(jnp.bfloat16)
    scores = (
        jnp.einsum("pqhd,pkhd->phqk", q, k, preferred_element_type=jnp.float32)
        + jnp.einsum("pqhc,pkc->phqk", box_query, box_keys, preferred_element_type=jnp.float32)
    ) * score_scale
    is_valid = (jnp.arange(page_len)[None, :] < page_lengths[:, None])[:, None, None, :]
    masked = jnp.where(is_valid, scores, MASKED)
    probs = jax.nn.softmax(masked, axis=-1)
    probs_low = probs.astype(jnp.bfloat16)
    mixed = jnp.einsum("phqk,pkhd->pqhd", probs_low, v, preferred_element_type=jnp.float32)
    mixed_low = mixed.astype(jnp.bfloat16).reshape(-1, model_width)
    unit1, inv1 = normalize(x.astype(jnp.float32) + dot32(mixed_low, full_out) + bo)
    y1 = unit1 * g1 + e1
    y1_low = y1.astype(jnp.bfloat16)
    pre = dot32(y1_low, full_up) + b1
    hidden = jax.nn.gelu(pre, approximate=False).astype(jnp.bfloat16)
    unit2, inv2 = normalize(y1 + dot32(hidden, full_down) + b2)
    output = (unit2 * g2 + e2).astype(jnp.bfloat16)

    seed = page_cotangent.reshape(-1, model_width).astype(jnp.float32)
    d_h2, d_g2, d_e2 = normalize_back(seed, unit2, inv2, g2)
    d_f = d_h2.astype(jnp.bfloat16)
    d_hidden = dot32(d_f, full_down.T)
    d_pre = jax.vjp(partial(jax.nn.gelu, approximate=False), pre)[1](d_hidden)[0]
    d_pre = d_pre.astype(jnp.bfloat16)
    d_wdown = dot32(hidden.T, d_f)
    d_wup = dot32(y1_low.T, d_pre)
    d_y1 = dot32(d_pre, full_up.T) + d_h2
    d_h1, d_g1, d_e1 = normalize_back(d_y1, unit1, inv1, g1)
    d_a = d_h1.astype(jnp.bfloat16)
    d_wout = dot32(mixed_low.T, d_a)
    d_mixed = dot32(d_a, full_out.T).astype(jnp.bfloat16).reshape(head_shape)
    row_delta = jnp.einsum("pqhd,pqhd->phq", d_mixed.astype(jnp.float32), mixed)
    d_probs = jnp.einsum("pqhd,pkhd->phqk", d_mixed, v, preferred_element_type=jnp.float32)
    d_raw = (probs * (d_probs - row_delta[..., None])).astype(jnp.bfloat16)
    d_q = jnp.einsum("phqk,pkhd->pqhd", d_raw, k, preferred_element_type=jnp.float32)
    d_box_q = jnp.einsum("phqk,pkc->pqhc", d_raw, box_keys, preferred_element_type=jnp.float32)
    d_k = jnp.einsum("phqk,pqhd->pkhd", d_raw, q, preferred_element_type=jnp.float32)
    d_v = jnp.einsum("phqk,pqhd->pkhd", probs_low, d_mixed, preferred_element_type=jnp.float32)
    d_coeffs = unrotate(d_box_q * score_scale, table).astype(jnp.bfloat16)
    d_q = d_q * score_scale + jnp.einsum(
        "pqhc,hdc->pqhd", d_coeffs, box_heads, preferred_element_type=jnp.float32
    )
    d_wbox = jnp.einsum("pqhd,pqhc->hdc", q, d_coeffs, preferred_element_type=jnp.float32)
    flat = (-1, model_width)
    d_q = d_q.astype(jnp.bfloat16).reshape(flat)
    d_k = (d_k * score_scale).astype(jnp.bfloat16).reshape(flat)
    d_v = d_v.astype(jnp.bfloat16).reshape(flat)
    d_c = jnp.concatenate([d_q, d_k, d_v], axis=1)
    d_wqkv = dot32(x.T, d_c)
    d_x = dot32(d_c, full_qkv.T) + d_h1
    total = partial(jnp.sum, axis=0, dtype=jnp.float32)
    vector_grad = jnp.concatenate(
        [total(d_q), total(d_v), total(d_a), d_g1, d_e1, total(d_pre), total(d_f), d_g2, d_e2]
    )
    return (
        from_pages(output.reshape(page_tokens.shape)),
        from_pages(d_x.reshape(page_tokens.shape)),
        scatter_weight(d_wqkv),
        scatter_weight(d_wbox.reshape(model_width, BOX_DIM)),
        scatter_weight(d_wout),
        scatter_weight(d_wup),
        scatter_weight(d_wdown),
        lax.psum_scatter(vector_grad, ("dp", "blk"), scatter_dimension=0, tiled=True),
    )


GATHER_GROUPS = (
    ("qkv", (0, 48, 0, 384), (("zxy", (0, 48, 0, 384)),)),
    ("qkv", (0, 48, 384, 384), (("yzx", (0, 48, 384, 256)), ("yzx", (0, 48, 640, 128)),)),
    ("qkv", (0, 48, 768, 384), (("zxy", (0, 48, 768, 384)),)),
    ("box", (0, 48, 0, 384), (("zxy", (0, 48, 0, 256)), ("yzx", (0, 48, 256, 128)),)),
    ("out", (0, 48, 0, 384), (("yxz", (0, 48, 0, 128)), ("xzy", (0, 48, 128, 256)),)),
    ("up", (0, 48, 0, 384), (("yxz", (0, 48, 0, 256)), ("zyx", (0, 48, 256, 128)),)),
    ("up", (0, 48, 384, 384), (("zyx", (0, 48, 384, 384)),)),
    ("up", (0, 48, 768, 384), (("yxz", (0, 48, 768, 384)),)),
    ("up", (0, 48, 1152, 384), (("zyx", (0, 48, 1152, 256)), ("zyx", (0, 48, 1408, 128)),)),
    ("down", (0, 192, 0, 128), (("zxy", (0, 64, 0, 128)), ("yxz", (64, 128, 0, 128)),)),
    ("down", (0, 192, 128, 128), (("zyx", (0, 64, 128, 128)), ("xzy", (64, 128, 128, 128)),)),
    ("down", (0, 192, 256, 128), (("zxy", (0, 192, 256, 128)),)),
)
GATHER_EVENTS = (
    (1, 0, 0, 0),
    (1, 1, 1, 0),
    (1, 2, 0, 0),
    (1, 3, 0, 0),
    (1, 0, 0, 10),
    (1, 0, 0, 1),
    (1, 6, 0, 0),
    (1, 3, 1, 0),
    (1, 5, 0, 0),
    (1, 8, 1, 0),
    (1, 2, 0, 10),
    (1, 4, 0, 0),
    (1, 1, 0, 0),
    (2, 9, 0, 0),
    (2, 3, 0, 10),
    (2, 7, 0, 0),
    (2, 2, 0, 1),
    (2, 9, 1, 0),
    (2, 1, 1, 1),
    (2, 8, 0, 0),
    (2, 0, 0, 2),
    (3, 1, 0, 1),
    (3, 3, 0, 1),
    (4, 7, 0, 1),
    (4, 1, 1, 11),
    (4, 3, 1, 1),
    (4, 4, 0, 1),
    (4, 2, 0, 2),
    (4, 9, 0, 10),
    (5, 5, 1, 0),
    (5, 10, 1, 0),
    (6, 4, 1, 0),
    (7, 1, 1, 2),
    (7, 6, 0, 10),
    (7, 1, 0, 11),
    (8, 3, 0, 2),
    (8, 9, 0, 1),
    (8, 3, 1, 11),
    (8, 11, 0, 0),
    (8, 10, 1, 1),
    (9, 8, 0, 10),
    (9, 8, 1, 10),
    (9, 1, 0, 2),
    (9, 6, 0, 1),
    (10, 0, 0, 3),
    (10, 1, 1, 3),
    (10, 0, 0, 4),
    (11, 5, 1, 10),
    (12, 10, 0, 0),
    (12, 3, 1, 2),
    (12, 2, 0, 3),
    (12, 9, 1, 1),
    (13, 5, 0, 1),
    (13, 11, 0, 10),
    (13, 10, 1, 11),
    (13, 4, 1, 1),
    (13, 8, 0, 1),
    (14, 1, 0, 3),
    (14, 4, 0, 2),
    (15, 5, 1, 1),
    (16, 8, 1, 1),
    (18, 1, 1, 4),
    (18, 2, 0, 4),
    (18, 9, 0, 2),
    (18, 1, 0, 4),
    (18, 11, 0, 1),
    (20, 3, 1, 3),
    (20, 10, 1, 2),
    (21, 3, 0, 3),
    (21, 4, 1, 11),
    (21, 5, 0, 2),
    (21, 7, 0, 2),
    (22, 10, 0, 10),
    (22, 3, 1, 4),
    (22, 9, 1, 2),
    (22, 6, 0, 2),
    (23, 3, 0, 4),
    (23, 8, 0, 2),
    (26, 4, 0, 12),
    (27, 5, 1, 2),
    (27, 10, 0, 1),
    (28, 4, 1, 2),
    (31, 11, 0, 2),
    (32, 10, 0, 2),
    (32, 5, 0, 12),
    (33, 7, 0, 12),
    (33, 4, 0, 3),
    (34, 6, 0, 3),
    (35, 9, 0, 3),
    (36, 8, 1, 2),
    (37, 4, 1, 3),
    (39, 10, 1, 3),
    (42, 8, 0, 3),
    (44, 6, 0, 4),
    (46, 5, 1, 3),
    (46, 9, 0, 4),
    (49, 4, 0, 4),
    (54, 10, 0, 3),
    (55, 5, 0, 3),
    (56, 4, 1, 4),
    (56, 7, 0, 3),
    (57, 10, 1, 4),
    (61, 5, 1, 4),
    (62, 8, 1, 3),
    (63, 10, 0, 4),
    (64, 9, 1, 12),
    (79, -1, 0, 0),
    (80, 5, 0, 4),
    (81, 11, 0, 3),
    (93, 7, 0, 4),
    (93, 8, 1, 4),
    (95, 9, 1, 3),
    (102, 8, 0, 4),
    (124, 9, 1, 4),
    (131, 11, 0, 4),
)
SCATTER_GROUPS = (
    ("down", "down", (0, 192, 0, 128), (0, 192, 0, 128), (("zxy", (0, 64, 0, 128)), ("xzy", (64, 128, 0, 128)),)),
    ("down", "down", (0, 192, 128, 128), (0, 192, 128, 128), (("zxy", (0, 64, 128, 128)), ("yxz", (64, 128, 128, 128)),)),
    ("down", "down", (0, 192, 256, 128), (0, 192, 256, 128), (("yzx", (0, 192, 256, 128)),)),
    ("up", "up", (0, 48, 0, 384), (0, 48, 0, 384), (("xyz", (0, 48, 0, 128)), ("yxz", (0, 48, 128, 256)),)),
    ("up", "up", (0, 48, 384, 384), (0, 48, 384, 384), (("xyz", (0, 48, 384, 384)),)),
    ("up", "up", (0, 48, 768, 384), (0, 48, 768, 384), (("xyz", (0, 48, 768, 384)),)),
    ("up", "up", (0, 48, 1152, 384), (0, 48, 1152, 384), (("xyz", (0, 48, 1152, 384)),)),
    ("out", "out", (0, 48, 0, 384), (0, 48, 0, 384), (("zyx", (0, 48, 0, 256)), ("yxz", (0, 48, 256, 128)),)),
    ("qkv", "early", (0, 48, 0, 384), 0, (("zxy", (0, 48, 0, 384)),)),
    ("box", "box", (0, 48, 0, 384), (0, 48, 0, 384), (("yxz", (0, 48, 0, 128)), ("xyz", (0, 48, 128, 256)),)),
    ("qkv", "down", (0, 48, 0, 384), 1, (("yxz", (0, 48, 0, 128)), ("yxz", (0, 48, 128, 256)),)),
    ("qkv", "down", (48, 48, 0, 384), 2, (("yxz", (48, 48, 0, 128)), ("xzy", (48, 48, 128, 256)),)),
)
SCATTER_EVENTS = (
    (4, 0, 0, 0),
    (6, 1, 0, 0),
    (12, 0, 0, 10),
    (12, 2, 0, 0),
    (15, 0, 1, 1),
    (15, 5, 0, 0),
    (16, 1, 0, 10),
    (17, 0, 1, 11),
    (17, 4, 0, 0),
    (18, 3, 0, 0),
    (19, 7, 0, 0),
    (19, -1, 0, 0),
    (22, 1, 0, 1),
    (24, 0, 0, 1),
    (24, 2, 0, 1),
    (24, 7, 0, 10),
    (25, 1, 1, 1),
    (27, 4, 0, 1),
    (31, 6, 0, 0),
    (32, 3, 1, 1),
    (32, 2, 0, 11),
    (34, 1, 1, 2),
    (35, 8, 0, 0),
    (35, 1, 0, 2),
    (36, 5, 0, 1),
    (38, 0, 1, 2),
    (39, 1, 1, 12),
    (41, 0, 0, 2),
    (41, 6, 0, 1),
    (41, 2, 0, 2),
    (45, 4, 0, 2),
    (45, 0, 1, 3),
    (46, 1, 1, 3),
    (46, 8, 0, 10),
    (46, 3, 0, 1),
    (47, 7, 0, 1),
    (47, 9, 0, 0),
    (47, 1, 0, 3),
    (47, 0, 0, 3),
    (47, 2, 0, 3),
    (48, 3, 1, 2),
    (48, -2, 0, 0),
    (48, 7, 1, 1),
    (48, 10, 0, 0),
    (49, 4, 0, 12),
    (49, 6, 0, 2),
    (49, 11, 0, 0),
    (50, 9, 1, 1),
    (51, 3, 0, 2),
    (62, 5, 0, 2),
    (64, 9, 0, 1),
    (67, -2, 0, 1),
    (68, 7, 0, 2),
    (71, 3, 0, 12),
    (78, 7, 1, 2),
    (89, 11, 1, 1),
    (98, 10, 1, 1),
    (100, 4, 0, 3),
    (117, -2, 0, 2),
    (128, 3, 0, 3),
    (183, 8, 0, 1),
    (521, 6, 0, 12),
    (525, 3, 1, 12),
    (544, 11, 1, 11),
    (563, 5, 0, 12),
    (615, 7, 1, 12),
    (874, 10, 0, 1),
    (912, 9, 0, 2),
    (918, 9, 1, 2),
    (959, 11, 0, 1),
    (959, 10, 0, 2),
    (975, 9, 1, 12),
    (978, 11, 0, 2),
    (979, 10, 1, 2),
    (979, 8, 0, 2),
    (999, 10, 0, 12),
    (1000, 11, 1, 2),
    (1002, 9, 0, 12),
    (1010, 3, 1, 3),
    (1020, 11, 0, 12),
    (1021, 9, 1, 3),
    (1032, 10, 0, 3),
    (1049, 10, 1, 12),
    (1059, 5, 0, 3),
    (1066, 11, 0, 3),
    (1068, 8, 0, 3),
    (1070, 7, 0, 3),
    (1073, 6, 0, 3),
    (1084, 9, 0, 3),
    (1095, 10, 1, 3),
    (1123, 11, 1, 3),
    (1148, 7, 1, 3),
)


MESH = pl.DeviceIdType.MESH
WEIGHTS = ("qkv", "box", "out", "up", "down")
ROT = 4
ALL = slice(None)


def window(piece):
    return (pl.ds(piece[0], piece[1]), pl.ds(piece[2], piece[3]))


class Place:
    def __init__(self):
        dp = lax.axis_index("dp")
        self.y = lax.axis_index("blk")
        self.z = lax.div(dp, 4)
        self.x = lax.rem(lax.div(dp, 2), 2)
        self.c = lax.rem(dp, 2)
        x, y, z, c = self.x, self.y, self.z, self.c
        self.near = z + 1 - 2 * lax.rem(z, 2)
        self.far = lax.rem(z + 2, 4)
        self.mirror = 3 - z
        self.inner = jnp.logical_or(z == 1, z == 2)
        self.end = jnp.logical_or(z == 0, z == 3)
        at = lambda other: (other * 4 + x * 2 + c, y)
        self.near_peer, self.far_peer, self.mirror_peer = at(self.near), at(self.far), at(self.mirror)
        self.x_peer = (dp + 2 - 4 * x, y)
        self.y_peer = (dp, 1 - y)
        self.c_peer = (dp + 1 - 2 * c, y)

    def own(self):
        return dict(y=self.y, z=self.z, x=self.x)

    def vector_offset(self):
        device = ((self.z * 2 + self.x) * 2 + self.c) * 2 + self.y
        return lax.rem(device * (VECTORS // 32), 128)

    def greet(self):
        barrier = pltpu.get_barrier_semaphore()
        peers = [self.near_peer, self.far_peer, self.mirror_peer]
        peers += [self.x_peer, self.y_peer, self.c_peer]
        for peer in peers:
            pl.semaphore_signal(barrier, inc=1, device_id=peer, device_id_type=MESH)
        pl.semaphore_wait(barrier, len(peers))


def semaphore_table(groups, slots):
    table = {}
    for g, group in enumerate(groups):
        for part, (path, _) in enumerate(group[-1]):
            for hop, axis in enumerate(path):
                for slot in range(slots if axis == "z" else 1):
                    table[g, part, hop, slot] = len(table)
    return table


SEND_RINGS = dict(all=(0, 24), inner=(24, 12), end=(36, 12))
SENDS = 48


class Sends:
    def __init__(self, place, events, started):
        self.place = place
        self.index, self.before, self.kind, self.after = {}, {}, {}, {}
        turns = {kind: [] for kind in SEND_RINGS}
        for at, (_, *event) in enumerate(events):
            for key, kind in started(*event):
                base, size = SEND_RINGS[kind]
                turn = turns[kind]
                self.index[key], self.kind[key] = base + len(turn) % size, kind
                if len(turn) >= size:
                    self.before[key] = turn[-size]
                    self.after[turn[-size]] = at
                turn.append(key)
        self.done = set()

    def when(self, key, act):
        kind = self.kind[key]
        if kind == "all":
            act()
        else:
            pl.when(self.place.inner if kind == "inner" else self.place.end)(act)

    def start(self, copy, *key):
        before = self.before.get(key)
        if before is not None and before not in self.done:
            copy(*before).wait_send()
        copy(*key).start()

    def left(self, copy, now=None, chosen=lambda key: True):
        for key in self.index:
            at = self.after.get(key)
            if key in self.done or not chosen(key) or (at is not None and (now is None or at < now)):
                continue
            self.done.add(key)
            self.when(key, copy(*key).wait_send)


def remote(src, dst, sems, at, peer, send=None):
    return pltpu.make_async_remote_copy(
        src,
        dst,
        sems[0].at[at if send is None else send],
        sems[1].at[at],
        device_id=peer,
        device_id_type=MESH,
    )


def core_table(groups):
    keys = [(g, part) for g, group in enumerate(groups) for part in range(len(group[-1]))]
    return {key: n for n, key in enumerate(keys)}


class Gather:
    def __init__(self, place, groups, shards, full, sems, own_sem):
        self.place, self.groups, self.shards, self.full = place, groups, shards, full
        self.sems, self.own_sem = sems, own_sem
        self.count = len(groups)
        self.table = semaphore_table(groups, 3)
        self.c_table = core_table(groups)
        self.sends = Sends(place, GATHER_EVENTS, self.started)
        self.owned = False

    def started(self, g, part, step):
        if g < 0 or step == 4:
            return []
        if step == 3:
            return [((g, part, 3, 0), "all")]
        if step >= 10:
            return [((g, part, step - 10, 3), "inner")]
        if self.groups[g][2][part][0][step] != "z":
            return [((g, part, step, 0), "all")]
        return [
            ((g, part, step, 1), "all"),
            ((g, part, step, 0), "all"),
            ((g, part, step, 2), "inner"),
        ]

    def copy(self, g, part, hop, slot, arriving=False):
        p = self.place
        name, _, parts = self.groups[g]
        path, piece = parts[part]
        cut = window(piece)
        send = self.sends.index[g, part, hop, slot]
        if hop == 3:
            c = 1 - p.c if arriving else p.c
            ref = self.full[name].at[(ALL, ALL, ALL, c) + cut]
            at = len(self.table) + self.c_table[g, part]
            return remote(ref, ref, self.sems, (at,), p.c_peer, (send,))
        axis = path[hop]
        at = p.own()
        at.update({earlier: ALL for earlier in path[:hop]})
        if axis == "z":
            peer = (p.near_peer, p.far_peer, p.mirror_peer, p.near_peer)[slot]
            if slot == 3:
                at["z"] = p.mirror if arriving else p.far
            elif arriving:
                at["z"] = (p.near, p.far, p.mirror)[slot]
        else:
            peer = p.x_peer if axis == "x" else p.y_peer
            if arriving:
                at[axis] = 1 - at[axis]
        ref = self.full[name].at[(at["y"], at["z"], at["x"], p.c) + cut]
        source = self.shards[name].at[cut] if hop == 0 and slot < 3 else ref
        at = self.table[g, part, hop, min(slot, 2)]
        return remote(source, ref, self.sems, (at,), peer, (send,))

    def own_copy(self, g):
        p = self.place
        name, both, _ = self.groups[g]
        cut = window(both)
        return pltpu.make_async_copy(
            self.shards[name].at[cut],
            self.full[name].at[(p.y, p.z, p.x, p.c) + cut],
            self.own_sem.at[g],
        )

    def relay(self, g, part, hop):
        @pl.when(self.place.inner)
        def _():
            self.copy(g, part, hop, 1, True).wait_recv()
            self.sends.start(self.copy, g, part, hop, 3)

    def start(self, g, part, hop):
        if self.groups[g][2][part][0][hop] != "z":
            self.sends.start(self.copy, g, part, hop, 0)
            return
        self.sends.start(self.copy, g, part, hop, 1)
        self.sends.start(self.copy, g, part, hop, 0)

        @pl.when(self.place.inner)
        def _():
            self.sends.start(self.copy, g, part, hop, 2)

    def finish(self, g, part, hop):
        self.copy(g, part, hop, 0, True).wait_recv()
        if self.groups[g][2][part][0][hop] != "z":
            return

        @pl.when(self.place.inner)
        def _():
            self.copy(g, part, hop, 2, True).wait_recv()

        @pl.when(self.place.end)
        def _():
            self.copy(g, part, hop, 1, True).wait_recv()
            self.copy(g, part, hop, 3, True).wait_recv()

    def own(self):
        for g in range(self.count):
            self.own_copy(g).start()

    def step(self, g, part, step):
        if step >= 10:
            self.relay(g, part, step - 10)
            return
        if step >= 1 and not self.owned:
            self.owned = True
            for other in range(self.count):
                self.own_copy(other).wait()
        if 1 <= step <= 3:
            self.finish(g, part, step - 1)
        if step <= 2:
            self.start(g, part, step)
        if step == 3:
            self.sends.start(self.copy, g, part, 3, 0)
        if step == 4:
            self.copy(g, part, 3, 0, True).wait_recv()


class Clock:
    def __init__(self, events, run, begun=None):
        self.events, self.run, self.now, self.at, self.begun = events, run, 0, 0, begun

    def may(self, event):
        return self.begun is None or event[1] < 0 or event[1] in self.begun

    def take(self):
        self.now += 1
        first = self.at
        while self.at < len(self.events):
            event = self.events[self.at]
            if event[0] > self.now or not self.may(event):
                break
            self.at += 1
        return self.events[first : self.at]

    def point(self):
        for _, *event in self.take():
            self.run(*event)

    def upto(self, *wanted):
        self.now += 1
        last = max(i for i, (_, *event) in enumerate(self.events) if tuple(event) in wanted)
        while self.at <= last:
            assert self.may(self.events[self.at])
            _, *event = self.events[self.at]
            self.at += 1
            self.run(*event)

    def loop(self, count, body, points=1):
        due = [[self.take() for _ in range(points)] for _ in range(count)]

        def wrapped(i, carry):
            point = iter(range(points))

            def serve():
                k = next(point)
                for n in range(count):
                    if due[n][k]:

                        @pl.when(i == n)
                        def _():
                            for _, *event in due[n][k]:
                                self.run(*event)

            serve()
            return body(i, carry, serve)

        lax.fori_loop(0, count, wrapped, 0)
        self.point()


def sine_cosine(angle):
    turns = jnp.floor(angle * (2.0 / math.pi) + 0.5)
    rest = angle - turns * 1.5703125
    rest = rest - turns * 4.837512969970703125e-4
    rest = rest - turns * 7.54978995489188216e-8
    square = rest * rest
    sine = rest + rest * square * (
        -1.6666654611e-1 + square * (8.3321608736e-3 + square * -1.9515295891e-4)
    )
    cosine = (
        1.0
        - 0.5 * square
        + square
        * square
        * (
            4.166664568298827e-2
            + square * (-1.388731625493765e-3 + square * 2.443315711809948e-5)
        )
    )
    quarter = turns.astype(jnp.int32)
    odd = (quarter & 1) == 1
    sine_sign = jnp.where((quarter & 2) == 2, -1.0, 1.0)
    cosine_sign = jnp.where(((quarter + 1) & 2) == 2, -1.0, 1.0)
    return (
        sine_sign * jnp.where(odd, cosine, sine),
        cosine_sign * jnp.where(odd, sine, cosine),
    )


def dot_t(a, b):
    return lax.dot_general(a, b, (((1,), (1,)), ((), ())), preferred_element_type=jnp.float32)


def dot_n(a, b):
    return lax.dot_general(a, b, (((0,), (0,)), ((), ())), preferred_element_type=jnp.float32)


def lanes(start, size):
    return pl.ds(pl.multiple_of(start, 128), size)


BQ, BV, BO, G1, E1, B1, B2, G2, E2 = 0, 768, 1536, 2304, 3072, 3840, 6912, 7680, 8448
VECTORS = 9216


def forward_kernel(plan, *refs):
    groups, page_len, width = plan
    block = page_len // 2
    refs = iter(refs)
    take = lambda n: [next(refs) for _ in range(n)]
    tokens, cotangent, boxes, lengths, vectors = take(5)
    shards = dict(zip(WEIGHTS, take(5)))
    full_out = dict(zip(WEIGHTS, take(5)))
    (x_out, ct_out, qkv_out, table_out, p_out, o_out, unit1_out, inv1_out) = take(8)
    (g_out, d_out, unit2_out, inv2_out, vec_out) = take(5)
    full = dict(zip(WEIGHTS, take(5)))
    (x_own, boxes_peer, pieces, vec, qkv, table, keys, box_w, p_slots, o_own, o_low) = take(11)
    (unit1, inv1, y1_low, hidden, slope, unit2, inv2) = take(7)
    w_sems = take(2)
    (own_sem,) = take(1)
    vz_sems, vxy_sems, vc_sems = take(2), take(2), take(2)
    ex_sems = take(2)
    (local_sem, p_sem, out_sem) = take(3)
    bias_qkv, piece = take(2)

    place = Place()
    y, z, x, c = place.y, place.z, place.x, place.c
    gather = Gather(place, groups, shards, full, w_sems, own_sem)

    def swap(i, source, target, arriving=False):
        at = (1 - y) if arriving else y
        return remote(
            source.at[1 - y], target.at[pl.ds(pl.multiple_of(at * block, block), block)],
            ex_sems, (i,), place.y_peer,
        )

    def keep(i, source, target):
        return pltpu.make_async_copy(
            source.at[y], target.at[pl.ds(pl.multiple_of(y * block, block), block)],
            local_sem.at[i],
        )

    box_swap = remote(boxes, boxes_peer, ex_sems, (2,), place.y_peer)

    def vector_y(arriving=False):
        at = 1 - y if arriving else y
        return remote(piece, pieces.at[at, z, x, c], vxy_sems, (0,), place.y_peer)

    def vector_x(arriving=False):
        ref = pieces.at[:, z, 1 - x if arriving else x, c]
        return remote(ref, ref, vxy_sems, (1,), place.x_peer)

    def vector_z(k, arriving=False):
        ref = pieces.at[:, lax.rem(z + 4 - k, 4) if arriving else z, :, c]
        peer = (lax.rem(z + k, 4) * 4 + x * 2 + c, y)
        return remote(ref, ref, vz_sems, (k - 1,), peer)

    def vector_c(arriving=False):
        ref = pieces.at[:, :, :, 1 - c if arriving else c]
        return remote(ref, ref, vc_sems, (0,), place.c_peer)

    vector_own = pltpu.make_async_copy(piece, pieces.at[y, z, x, c], local_sem.at[2])

    def event(g, part, step):
        if g < 0:
            swap(1, cotangent, ct_out).start()
        else:
            gather.step(g, part, step)

    clock = Clock(GATHER_EVENTS, event)

    def need(g):
        clock.upto(*((g, part, 4) for part in range(len(groups[g][2]))))

    outgoing = []

    def send_out(ref, out):
        copy = pltpu.make_async_copy(ref, out, out_sem.at[len(outgoing)])
        copy.start()
        outgoing.append(copy)

    own_vector = vectors[...].astype(jnp.float32).reshape(1, -1)
    own_vector = jnp.concatenate(
        [own_vector, jnp.zeros((1, 384 - own_vector.shape[1]), jnp.float32)], axis=1
    )
    own_vector = jnp.broadcast_to(own_vector, (8, 384))
    piece[...] = pltpu.roll(own_vector, place.vector_offset(), 1)[0:1, :]
    place.greet()
    gather.own()
    box_swap.start()
    vector_y().start()
    vector_own.start()
    swap(0, tokens, x_own).start()
    clock.point()
    keep(0, tokens, x_own).start()
    keep(1, cotangent, ct_out).start()

    box_swap.wait_recv()
    mine, other = boxes[...], boxes_peer[...]
    first_block = y == 0
    mine = jnp.where(first_block, mine[:, 0, :], mine[:, 1, :])
    other = jnp.where(first_block, other[:, 0, :], other[:, 1, :])
    both = jnp.concatenate(
        [jnp.where(first_block, mine, other), jnp.where(first_block, other, mine)], axis=1
    ).astype(jnp.float32)
    both = jnp.concatenate([both, jnp.zeros((6, page_len), jnp.float32)], axis=0)
    across_up = both.T
    lane = lax.broadcasted_iota(jnp.int32, (1, 2 * FREQ), 1)
    step = jnp.where(lane < FREQ, lane, lane - FREQ).astype(jnp.float32)
    frequency = jnp.exp(step * (-math.log(10000.0) / FREQ))
    angle = jnp.where(lane < FREQ, across_up[:, 0:1], across_up[:, 1:2]) * frequency
    sine, cosine = sine_cosine(angle)
    table[0], table[1] = cosine, sine
    keys[0 : 2 * FREQ, :] = cosine.astype(jnp.bfloat16).T
    keys[2 * FREQ :, :] = sine.astype(jnp.bfloat16).T
    send_out(table, table_out)
    clock.point()
    vector_own.wait()
    vector_y(True).wait_recv()
    vector_x().start()
    clock.point()
    vector_x(True).wait_recv()
    for k in range(1, 4):
        vector_z(k).start()
    clock.point()
    clock.upto(*((0, part, 3) for part in range(len(groups[0][2]))))
    for k in range(1, 4):
        vector_z(k, True).wait_recv()
    vector_c().start()
    need(0)
    vector_c(True).wait_recv()
    vec[...] = jnp.zeros_like(vec)
    for dz in range(4):
        for dx in range(2):
            for dc in range(2):
                for dy in range(2):
                    device = ((dz * 2 + dx) * 2 + dc) * 2 + dy
                    start = device * (VECTORS // 32) // 128 * 128
                    vec[:, start : start + 384] += pieces[dy, dz, dx, dc]
    send_out(vec, vec_out)

    def vector(start, size=width):
        return vec[:, start : start + size]

    def project(first, count):
        def project_tile(h, carry):
            w = full["qkv"].at[h][:, :, :, :, first : first + count].reshape(width, count)
            out = jnp.dot(x_own[...], w, preferred_element_type=jnp.float32)
            start = pl.multiple_of(h * 1152 + first, 128)
            column = start + lax.broadcasted_iota(jnp.int32, (1, count), 1)
            bias = bias_qkv[:, lanes(start, count)]
            qkv[:, lanes(start, count)] = (out + bias).astype(jnp.bfloat16)
            return carry

        lax.fori_loop(0, 2, project_tile, 0)

    bias_qkv[:, 0:width] = vector(BQ)
    bias_qkv[:, width : 2 * width] = jnp.zeros((1, width), jnp.float32)
    bias_qkv[:, 2 * width : 3 * width] = vector(BV)
    for g, (name, cut, _) in enumerate(groups):
        if name == "qkv":
            if g == 0:
                keep(0, tokens, x_own).wait()
                swap(0, tokens, x_own, True).wait_recv()
                send_out(x_own, x_out)
            else:
                need(g)
            project(cut[2], cut[3])
            clock.point()
    send_out(qkv, qkv_out)

    box_group = [g for g, group in enumerate(groups) if group[0] == "box"][-1]
    need(box_group)
    low = full["box"].at[0][...].reshape(width, 2 * FREQ)
    high = full["box"].at[1][...].reshape(width, 2 * FREQ)
    box_w[...] = jnp.concatenate(
        [low[:, :FREQ], high[:, :FREQ], low[:, FREQ:], high[:, FREQ:]], axis=1
    )
    page_length = jnp.where(first_block, lengths[0], lengths[1])
    valid = lax.broadcasted_iota(jnp.int32, (1, page_len), 1) < page_length
    head_lane = lax.broadcasted_iota(jnp.int32, (1, 128), 1)

    def p_copy(p, slot):
        return pltpu.make_async_copy(p_slots.at[slot], p_out.at[p], p_sem.at[slot])

    def pair(p, carry, serve):
        slot = lax.rem(p, 2)

        @pl.when(p >= 2)
        def _():
            p_copy(p - 2, slot).wait()

        q = qkv[:, lanes(p * 128, 128)]
        k = qkv[:, lanes(width + p * 128, 128)].T
        v = qkv[:, lanes(2 * width + p * 128, 128)]
        w = box_w[pl.ds(pl.multiple_of(p * 128, 128), 128), :]
        outs = []
        for i in range(2):
            if i:
                serve()
            of_head = (head_lane < HEAD) == (i == 0)
            q_head = jnp.where(of_head, q, jnp.zeros_like(q))
            u = jnp.dot(q_head, w, preferred_element_type=jnp.float32)
            on_sine, on_cosine = u[:, : 2 * FREQ], u[:, 2 * FREQ :]
            cosine, sine = table[0], table[1]
            b_cosine = (on_sine * sine + on_cosine * cosine).astype(jnp.bfloat16)
            b_sine = (on_cosine * sine - on_sine * cosine).astype(jnp.bfloat16)
            serve()
            b = jnp.concatenate([q_head, b_cosine, b_sine], axis=1)
            s = jnp.dot(b, jnp.concatenate([k, keys[...]], axis=0), preferred_element_type=jnp.float32)
            s = jnp.where(valid, s, MASKED)
            top = jnp.max(s, axis=1, keepdims=True)
            e = jnp.exp((s - top) * (HEAD**-0.5))
            probs = (e * (1.0 / jnp.sum(e, axis=1, keepdims=True))).astype(jnp.bfloat16)
            p_slots[slot, i] = probs
            outs.append(jnp.dot(probs, v, preferred_element_type=jnp.float32))
        mixed = jnp.where(head_lane < HEAD, outs[0], outs[1])
        o_own[:, lanes(p * 128, 128)] = mixed
        o_low[:, lanes(p * 128, 128)] = mixed.astype(jnp.bfloat16)
        p_copy(p, slot).start()
        return carry

    clock.loop(HEADS // 2, pair, 4)
    p_copy(4, 0).wait()
    p_copy(5, 1).wait()
    send_out(o_own, o_out)

    def last_of(name):
        return [g for g, group in enumerate(groups) if group[0] == name][-1]

    def weight_out(name):
        send_out(full[name], full_out[name])

    weight_out("qkv")
    weight_out("box")
    need(last_of("out"))
    weight_out("out")
    for h in range(2):
        w = full["out"].at[h][...].reshape(width, 384)
        cut = slice(h * 384, (h + 1) * 384)
        o_own_part = jnp.dot(o_low[...], w, preferred_element_type=jnp.float32)
        unit2[:, cut] = x_own[:, cut].astype(jnp.float32) + o_own_part + vec[:, BO + h * 384 : BO + (h + 1) * 384]

    def norm(hidden_sum):
        mean = jnp.mean(hidden_sum, axis=1, keepdims=True)
        centered = hidden_sum - mean
        inverse = lax.rsqrt(jnp.mean(centered * centered, axis=1, keepdims=True) + EPSILON)
        return centered * inverse, inverse

    unit, inverse = norm(unit2[...])
    unit1[...] = unit
    inv1[...] = jnp.broadcast_to(inverse, (page_len, 128))
    y1 = unit * vector(G1) + vector(E1)
    y1_low[...] = y1.astype(jnp.bfloat16)
    unit2[...] = y1 + vector(B2)
    send_out(unit1, unit1_out)
    send_out(inv1, inv1_out)

    def up_tile(first, h, t):
        start = pl.multiple_of(first + t * UP_TILE, 128)
        w = full["up"].at[h][:, :, :, :, pl.ds(start, UP_TILE)].reshape(width, UP_TILE)
        at = lanes(h * 1536 + start, UP_TILE)
        pre = jnp.dot(y1_low[...], w, preferred_element_type=jnp.float32)
        pre = pre + vec[:, lanes(B1 + h * 1536 + start, UP_TILE)]
        half = 0.5 + 0.5 * lax.erf(pre * (2.0**-0.5))
        hidden[:, at] = (pre * half).astype(jnp.bfloat16)
        bell = jnp.exp(pre * pre * -0.5) * ((2.0 * math.pi) ** -0.5)
        slope[:, at] = (half + pre * bell).astype(jnp.bfloat16)

    clock.point()
    for g, (name, cut, _) in enumerate(groups):
        if name == "up":
            need(g)
            tiles = cut[3] // UP_TILE

            def up_body(i, carry, first=cut[2], tiles=tiles):
                up_tile(first, lax.div(i, tiles), lax.rem(i, tiles))
                return carry

            lax.fori_loop(0, 2 * tiles, up_body, 0)
            clock.point()
    send_out(hidden, g_out)
    send_out(slope, d_out)
    weight_out("up")

    for g, (name, cut, _) in enumerate(groups):
        if name == "down":
            need(g)
            first, count = cut[2], cut[3]
            columns = (ALL,) * 4 + window(cut)
            send_out(full["down"].at[columns], full_out["down"].at[columns])

            def down_body(h, carry, first=first, count=count):
                w = full["down"].at[h][:, :, :, :, first : first + count].reshape(4 * width, count)
                at = lanes(h * 384 + first, count)
                unit2[:, at] += jnp.dot(hidden[...], w, preferred_element_type=jnp.float32)
                return carry

            lax.fori_loop(0, 2, down_body, 0)
            clock.point()
    clock.upto(*(tuple(event) for _, *event in GATHER_EVENTS))
    unit, inverse = norm(unit2[...])
    unit2[...] = unit
    inv2[...] = jnp.broadcast_to(inverse, (page_len, 128))
    send_out(unit2, unit2_out)
    send_out(inv2, inv2_out)

    gather.sends.left(gather.copy)
    for k in range(1, 4):
        vector_z(k).wait_send()
    vector_y().wait_send()
    vector_x().wait_send()
    vector_c().wait_send()
    box_swap.wait_send()
    swap(0, tokens, x_own).wait_send()
    swap(1, cotangent, ct_out).wait_send()
    swap(1, cotangent, ct_out, True).wait_recv()
    keep(1, cotangent, ct_out).wait()
    for copy in outgoing:
        copy.wait()


UP_TILE = 384


def forward_call(tokens, cotangent, boxes, lengths, vectors, shards):
    page_len = tokens.shape[1] * 2
    width = tokens.shape[2]
    groups = GATHER_GROUPS
    count = len(groups)
    full = [jax.ShapeDtypeStruct((2, 4, 2, 2) + s.shape, jnp.bfloat16) for s in shards]
    low, single = jnp.bfloat16, jnp.float32
    kinds = dict(
        x=((page_len, width), low),
        ct=((page_len, width), low),
        qkv=((page_len, 3 * width), low),
        table=((2, page_len, 2 * FREQ), single),
        p=((HEADS // 2, 2, page_len, page_len), low),
        o=((page_len, width), single),
        unit1=((page_len, width), single),
        inv1=((page_len, 128), single),
        g=((page_len, 4 * width), low),
        d=((page_len, 4 * width), low),
        unit2=((page_len, width), single),
        inv2=((page_len, 128), single),
        vec=((1, VECTORS + 128), single),
    )
    outs = full + [jax.ShapeDtypeStruct(*kinds[k]) for k in kinds]
    anywhere = pl.BlockSpec(memory_space=pl.ANY)
    vmem = pl.BlockSpec(memory_space=pltpu.VMEM)
    smem = pl.BlockSpec(memory_space=pltpu.SMEM)
    dma = pltpu.SemaphoreType.DMA
    scratch = [pltpu.VMEM(f.shape, f.dtype) for f in full]
    scratch += [
        pltpu.VMEM((page_len, width), low),
        pltpu.VMEM(boxes.shape, jnp.int32),
        pltpu.VMEM((2, 4, 2, 2, 1, 384), single),
        pltpu.VMEM((1, VECTORS + 128), single),
        pltpu.VMEM((page_len, 3 * width), low),
        pltpu.VMEM((2, page_len, 2 * FREQ), single),
        pltpu.VMEM((BOX_DIM, page_len), low),
        pltpu.VMEM((width, BOX_DIM), low),
        pltpu.VMEM((2, 2, page_len, page_len), low),
        pltpu.VMEM((page_len, width), single),
        pltpu.VMEM((page_len, width), low),
        pltpu.VMEM((page_len, width), single),
        pltpu.VMEM((page_len, 128), single),
        pltpu.VMEM((page_len, width), low),
        pltpu.VMEM((page_len, 4 * width), low),
        pltpu.VMEM((page_len, 4 * width), low),
        pltpu.VMEM((page_len, width), single),
        pltpu.VMEM((page_len, 128), single),
    ]
    arrivals = len(semaphore_table(groups, 3)) + len(core_table(groups))
    scratch += [dma((SENDS,)), dma((arrivals,))]
    scratch += [dma((count,))]
    scratch += [dma((3,))] * 2 + [dma((2,))] * 2 + [dma((1,))] * 2
    scratch += [dma((3,))] * 2 + [dma((3,)), dma((2,)), dma((20,))]
    scratch += [pltpu.VMEM((1, 3 * width), single), pltpu.VMEM((1, 384), single)]
    plan = (groups, page_len, width)
    results = pl.pallas_call(
        partial(forward_kernel, plan),
        out_shape=outs,
        in_specs=[anywhere, anywhere, vmem, smem, vmem] + [anywhere] * 5,
        out_specs=[anywhere] * len(outs),
        scratch_shapes=scratch,
        compiler_params=pltpu.CompilerParams(
            collective_id=0, has_side_effects=True, vmem_limit_bytes=VMEM_LIMIT
        ),
    )(tokens, cotangent, boxes, lengths, vectors, *shards)
    return dict(zip(WEIGHTS, results[:5])), dict(zip(kinds, results[5:]))


VMEM_LIMIT = 60 * 2**20


def landing_shape(path, hop, piece):
    sizes = dict(y=2, z=4, x=2)
    to_come = [sizes[axis] for axis in "yzx" if axis in path[hop + 1 :]]
    return (4 if path[hop] == "z" else 1, *to_come, piece[1], piece[3])


THIRDS = ((0, 1, 2), (1, 0, 2))


class Scatter:
    def __init__(self, place, groups, stored, c_land, landing, summed, sems, c_sems):
        self.place, self.groups, self.stored, self.summed = place, groups, stored, summed
        self.c_land, self.landing = c_land, landing
        self.sems, self.c_sems = sems, c_sems
        self.table = semaphore_table(groups, 4)
        self.sends = Sends(place, SCATTER_EVENTS, self.started)
        self.sent = set()

    def started(self, g, part, step):
        if g < 0 or step == 3:
            return []
        if step >= 10:
            return [((g, part, step - 10, 1), "inner")]
        out = []
        for other in range(len(self.groups[g][-1])) if step == 0 else (part,):
            if self.groups[g][-1][other][0][step] != "z":
                out.append(((g, other, step, 0), "all"))
                continue
            out.append(((g, other, step, 3), "end"))
            out.append(((g, other, step, "end"), "end"))
            out.append(((g, other, step, 0), "all"))
            out.append(((g, other, step, 2), "inner"))
        return out

    def c_copy(self, g):
        p = self.place
        store, both = self.groups[g][1], self.groups[g][2]
        ref = self.stored[store].at[(ALL, ALL, ALL, 1 - p.c) + window(both)]
        return remote(ref, self.c_land[g], self.c_sems, (g,), p.c_peer)

    def copy(self, g, part, hop, slot):
        p = self.place
        send = self.sends.index[g, part, hop, slot]
        slot = 1 if slot == "end" else slot
        path, piece = self.groups[g][-1][part]
        axis = path[hop]
        at = p.own()
        at.update({later: ALL for later in path[hop + 1 :]})
        if axis == "z":
            at["z"] = (p.near, p.far, p.mirror, p.mirror)[slot]
            peer = (p.near_peer, p.far_peer, p.mirror_peer, p.near_peer)[slot]
        else:
            at[axis] = 1 - at[axis]
            peer = p.x_peer if axis == "x" else p.y_peer
        ref = self.stored[self.groups[g][1]].at[(at["y"], at["z"], at["x"], p.c) + window(piece)]
        land = self.landing[g][part][hop].at[slot]
        at = self.table[g, part, hop, slot]
        return remote(ref, land, self.sems, (at,), peer, (send,))

    def add(self, g, part, hop, slots, place_z=None):
        p = self.place
        name, store, both, result, parts = self.groups[g]
        store = self.stored[store]
        path, piece = ("yzx", both) if hop < 0 else parts[part]
        cut = window(piece)
        sizes = dict(y=2, z=4, x=2)
        to_come = [axis for axis in "yzx" if axis in path[hop + 1 :]]
        count = math.prod(sizes[axis] for axis in to_come)
        land = self.c_land[g] if hop < 0 else self.landing[g][part][hop]

        def block(i):
            at = p.own()
            if place_z is not None:
                at["z"] = place_z
            inner = []
            for axis in to_come[::-1]:
                at[axis] = lax.rem(i, sizes[axis])
                i = lax.div(i, sizes[axis])
                inner.insert(0, at[axis])
            here = (at["y"], at["z"], at["x"], p.c) + cut
            arrived = [land[tuple(inner)] if hop < 0 else land[(slot, *inner)] for slot in slots]
            if len(arrived) == 1 and not (hop == 2 and place_z is None):
                return here, store[here] + arrived[0]
            value = store[here].astype(jnp.float32)
            for other in arrived:
                value = value + other.astype(jnp.float32)
            return here, value

        if hop == 2 and place_z is None:
            _, value = block(0)
            top, height, first, size = piece
            if name == "qkv":
                third = jnp.where(p.y == 0, THIRDS[0][result], THIRDS[1][result])
                self.summed[name][:, lanes(first + 384 * third, size)] = value
                return
            top, first = top - both[0] + result[0], first - both[2] + result[2]
            self.summed[name][top : top + height, first : first + size] = value
            return

        together = min(count, 4)

        def body(i, carry):
            for k in range(together):
                here, value = block(i * together + k)
                store[here] = value.astype(jnp.bfloat16)
            return carry

        lax.fori_loop(0, count // together, body, 0)

    def begin(self, g):
        self.c_copy(g).start()

    def start(self, g, part, hop):
        p = self.place
        if self.groups[g][-1][part][0][hop] != "z":
            self.sends.start(self.copy, g, part, hop, 0)
            return

        @pl.when(p.end)
        def _():
            self.sends.start(self.copy, g, part, hop, 3)
            self.sends.start(self.copy, g, part, hop, "end")

        self.sends.start(self.copy, g, part, hop, 0)

        @pl.when(p.inner)
        def _():
            self.sends.start(self.copy, g, part, hop, 2)

    def relay(self, g, part, hop):
        p = self.place

        @pl.when(p.inner)
        def _():
            self.copy(g, part, hop, 3).wait_recv()
            self.add(g, part, hop, (3,), p.far)
            self.sends.start(self.copy, g, part, hop, 1)

    def finish(self, g, part, hop):
        p = self.place
        self.copy(g, part, hop, 0).wait_recv()
        if self.groups[g][-1][part][0][hop] != "z":
            self.add(g, part, hop, (0,))
            return
        self.copy(g, part, hop, 1).wait_recv()

        @pl.when(p.inner)
        def _():
            self.copy(g, part, hop, 2).wait_recv()
            self.add(g, part, hop, (0, 1, 2))

        @pl.when(p.end)
        def _():
            self.add(g, part, hop, (0, 1))

    def step(self, g, part, step):
        if step >= 10:
            self.relay(g, part, step - 10)
            return
        if step == 0:
            self.c_copy(g).wait_recv()
            self.add(g, 0, -1, (0,))
            for part in range(len(self.groups[g][-1])):
                self.start(g, part, 0)
            return
        self.finish(g, part, step - 1)
        if step < 3:
            self.start(g, part, step)

    def left(self, chosen, now=None):
        for g in chosen:
            if g not in self.sent:
                self.sent.add(g)
                self.c_copy(g).wait_send()
        self.sends.left(self.copy, now, lambda key: key[0] in chosen)


def backward_kernel(plan, *refs):
    groups, page_len, width = plan
    block = page_len // 2
    refs = iter(refs)
    take = lambda n: [next(refs) for _ in range(n)]
    w_in = dict(zip(WEIGHTS, take(5)))
    (x_in, ct_in, qkv_in, table_in, p_in, o_in, unit1_in, inv1_in) = take(8)
    (g_in, d_in, unit2_in, inv2_in, vec_in) = take(5)
    out_out, dx_out = take(2)
    grad_out = dict(zip(WEIGHTS, take(5)))
    (piece_out,) = take(1)
    stored = dict(zip(("box", "out", "up", "down"), take(4)))
    count = len(groups)
    c_land = take(count)
    landing = [[take(3) for _ in group[-1]] for group in groups]
    summed = dict(zip(WEIGHTS, take(5)))
    w_box, w_out, box_w, box_g = take(4)
    (ct, qkv, table, keys, o_own, unit1, inv1, hidden, slope, unit2, inv2, vec) = take(12)
    (y1_low, d_a, d_mixed, out_low, dx_low, vec_g) = take(6)
    pieces, pc_land, py_land, px_land, pz_land, piece_sum = take(6)
    w_sems, c_sems = take(2), take(2)
    v_sems, vz_sems, ex_sems = take(2), take(2), take(2)
    in_sem, p_sem, out_sem = take(3)

    place = Place()
    y, z, x, c = place.y, place.z, place.x, place.c
    scatter = Scatter(place, groups, stored, c_land, landing, summed, w_sems, c_sems)

    sources = dict(
        unit2=(unit2_in, unit2),
        ct=(ct_in, ct),
        inv2=(inv2_in, inv2),
        vec=(vec_in, vec),
        g=(g_in, hidden),
        d=(d_in, slope),
        unit1=(unit1_in, unit1),
        inv1=(inv1_in, inv1),
        w_out=(w_in["out"], w_out),
        w_box=(w_in["box"], w_box),
        o=(o_in, o_own),
        qkv=(qkv_in, qkv),
        table=(table_in, table),
        x=(x_in, y1_low),
    )
    order = list(sources)

    def fetch(name):
        source, target = sources[name]
        return pltpu.make_async_copy(source, target, in_sem.at[order.index(name)])

    def fetch_weight(name, target):
        at = len(order) + ("down", "up", "qkv").index(name)
        return pltpu.make_async_copy(w_in[name], target, in_sem.at[at])

    def vector(start, size=width):
        return vec[:, start : start + size]

    def total(value):
        return jnp.sum(value.astype(jnp.float32), axis=0, keepdims=True)

    def norm_back(grad, unit, inverse, gain):
        scaled = grad * gain
        mean_grad = jnp.mean(scaled, axis=1, keepdims=True)
        mean_unit = jnp.mean(scaled * unit, axis=1, keepdims=True)
        return inverse * (scaled - mean_grad - unit * mean_unit)

    names = [group[0] for group in groups]

    def event(g, part, step):
        if g == -2:
            vector_step(step)
        elif g < 0:
            out_swap.start()
        else:
            scatter.step(g, part, step)

    clock = Clock(SCATTER_EVENTS, event, set())

    def begin(g):
        clock.begun.add(g)
        scatter.begin(g)

    for name in ("unit2", "ct", "inv2", "vec", "g"):
        fetch(name).start()
    place.greet()

    fetch("unit2").wait()
    fetch("ct").wait()
    fetch("inv2").wait()
    fetch("vec").wait()
    unit = unit2[...]
    out_low[...] = (unit * vector(G2) + vector(E2)).astype(jnp.bfloat16)
    seed = ct[...].astype(jnp.float32)
    vec_g[:, G2 : G2 + width] = total(seed * unit)
    vec_g[:, E2 : E2 + width] = total(seed)
    d_h2 = norm_back(seed, unit, inv2[:, 0:1], vector(G2))
    unit2[...] = d_h2
    ct[...] = d_h2.astype(jnp.bfloat16)
    d_f = ct
    vec_g[:, B2 : B2 + width] = total(d_f[...])

    def rows(at):
        return pl.ds(pl.multiple_of(at * block, block), block)

    out_swap = remote(out_low.at[rows(1 - y)], out_out.at[y], ex_sems, (0,), place.y_peer)
    out_keep = pltpu.make_async_copy(out_low.at[rows(y)], out_out.at[y], out_sem.at[0])
    dx_swap = remote(dx_low.at[0], dx_low.at[1], ex_sems, (1,), place.y_peer)

    def with_down(w_down):
        fetch_weight("down", w_down).start()
        fetch("g").wait()

        for name in ("d", "unit1", "inv1", "w_out", "o", "w_box", "qkv", "table"):
            fetch(name).start()

        def down_grads(first, size):
            left = d_f[:, first : first + size]
            right = d_f[:, 384 + first : 384 + first + size]
            both = jnp.concatenate([left, right], axis=1)

            def grad_tile(t, carry):
                part = dot_n(hidden[:, lanes(t * width, width)], both).astype(jnp.bfloat16)
                for h in range(2):
                    stored["down"][h, t, :, :, :, first : first + size] = part[
                        :, h * size : (h + 1) * size
                    ].reshape(2, 2, -1, size)
                return carry

            lax.fori_loop(0, 4, grad_tile, 0)
            for g, group in enumerate(groups):
                if group[0] == "down" and first <= group[2][2] < first + size:
                    begin(g)
            clock.point()

        down_grads(0, 128)
        down_grads(128, 256)
        out_keep.start()
        fetch_weight("down", w_down).wait()
        fetch("d").wait()

        def slope_tile(t, carry, serve):
            w0 = w_down.at[0, t][...].reshape(width, 384)
            w1 = w_down.at[1, t][...].reshape(width, 384)
            d_hidden = dot_t(d_f[...], jnp.concatenate([w0, w1], axis=1))
            at = lanes(t * width, width)
            d_pre = (d_hidden * slope[:, at].astype(jnp.float32)).astype(jnp.bfloat16)
            slope[:, at] = d_pre
            vec_g[:, lanes(B1 + t * width, width)] = total(d_pre)
            return carry

        clock.loop(4, slope_tile)

    pl.run_scoped(with_down, pltpu.VMEM(w_in["down"].shape, jnp.bfloat16))

    fetch("unit1").wait()
    fetch("inv1").wait()
    y1_low[...] = (unit1[...] * vector(G1) + vector(E1)).astype(jnp.bfloat16)

    def with_up(w_up):
        fetch_weight("up", w_up).start()

        def up_tile(i, carry, serve, part):
            tile = dot_n(y1_low[...], slope[:, lanes(i * 1536 + part * width, width)])
            stored["up"][i, :, :, :, :, part * width : (part + 1) * width] = tile.astype(
                jnp.bfloat16
            ).reshape(4, 2, 2, -1, width)
            return carry

        for part in range(2):
            clock.loop(2, partial(up_tile, part=part))
            for g, group in enumerate(groups):
                if group[0] == "up" and group[2][2] // width == part:
                    begin(g)
        fetch_weight("up", w_up).wait()

        def back_tile(h, carry, serve):
            w = w_up.at[h][...].reshape(width, 1536)
            unit2[...] += dot_t(slope[:, lanes(h * 1536, 1536)], w)
            return carry

        clock.loop(2, back_tile)

    pl.run_scoped(with_up, pltpu.VMEM(w_in["up"].shape, jnp.bfloat16))

    x_own = y1_low
    fetch("x").start()
    unit = unit1[...]
    d_y1 = unit2[...]
    vec_g[:, G1 : G1 + width] = total(d_y1 * unit)
    vec_g[:, E1 : E1 + width] = total(d_y1)
    d_h1 = norm_back(d_y1, unit, inv1[:, 0:1], vector(G1))
    unit1[...] = d_h1
    d_a[...] = d_h1.astype(jnp.bfloat16)
    vec_g[:, BO : BO + width] = total(d_a[...])
    fetch("w_out").wait()
    fetch("o").wait()
    both = jnp.concatenate([w_out.at[h][...].reshape(width, 384) for h in range(2)], axis=1)
    d_mixed[...] = dot_t(d_a[...], both).astype(jnp.bfloat16)
    part = dot_n(o_own[...].astype(jnp.bfloat16), d_a[...]).astype(jnp.bfloat16)
    for h in range(2):
        stored["out"][h] = part[:, h * 384 : (h + 1) * 384].reshape(4, 2, 2, -1, 384)
    begin(names.index("out"))
    clock.point()

    for name in ("w_box", "qkv", "table", "x"):
        fetch(name).wait()
    low = w_box.at[0][...].reshape(width, 2 * FREQ)
    high = w_box.at[1][...].reshape(width, 2 * FREQ)
    box_w[...] = jnp.concatenate(
        [low[:, :FREQ], high[:, :FREQ], low[:, FREQ:], high[:, FREQ:]], axis=1
    ).T
    keys[:, : 2 * FREQ] = table[0].astype(jnp.bfloat16)
    keys[:, 2 * FREQ :] = table[1].astype(jnp.bfloat16)
    table[...] = table[...] * (HEAD**-0.5)
    head_lane = lax.broadcasted_iota(jnp.int32, (1, 128), 1)

    def p_copy(p, slot, i):
        at = lanes((slot * 2 + i) * page_len, page_len)
        return pltpu.make_async_copy(p_in.at[p, i], hidden.at[:, at], p_sem.at[slot, i])

    p_copy(0, 0, 0).start()
    p_copy(0, 0, 1).start()

    vector_c = remote(pieces.at[:, :, :, 1 - c], pc_land, v_sems, (0,), place.c_peer)
    vector_y = remote(pieces.at[1 - y, :, :, c], py_land, v_sems, (1,), place.y_peer)
    vector_x = remote(pieces.at[y, :, 1 - x, c], px_land, v_sems, (2,), place.x_peer)

    def vector_z(k):
        there = lax.rem(z + k + 1, 4)
        peer = (there * 4 + x * 2 + c, y)
        return remote(pieces.at[y, there, x, c], pz_land.at[k], vz_sems, (k,), peer)

    def vector_step(step):
        if step == 0:
            vector_c.wait_recv()
            pieces[:, :, :, c] += pc_land[...]
            vector_y.start()
        if step == 1:
            vector_y.wait_recv()
            pieces[y, :, :, c] += py_land[...]
            vector_x.start()
        if step == 2:
            vector_x.wait_recv()
            pieces[y, :, x, c] += px_land[...]
            for k in range(3):
                vector_z(k).start()

    def with_qkv(w_qkv, early):
        stored["early"] = early
        fetch_weight("qkv", w_qkv).start()

        def pair(p, carry, serve):
            slot = lax.rem(p, 2)

            @pl.when(p < HEADS // 2 - 1)
            def _():
                p_copy(p + 1, 1 - slot, 0).start()
                p_copy(p + 1, 1 - slot, 1).start()

            p_copy(p, slot, 0).wait()
            p_copy(p, slot, 1).wait()
            q_t = qkv[:, lanes(p * 128, 128)].T
            k = qkv[:, lanes(width + p * 128, 128)]
            v_t = qkv[:, lanes(2 * width + p * 128, 128)].T
            w_t = box_w[:, lanes(p * 128, 128)]
            d_o = d_mixed[:, lanes(p * 128, 128)]
            d_o_t = d_o.T
            weighted = d_o.astype(jnp.float32) * o_own[:, lanes(p * 128, 128)]
            keys_k = jnp.concatenate([keys[...], k], axis=1)
            grads = []
            for i in range(2):
                if i:
                    serve()
                of_head = (head_lane < HEAD) == (i == 0)
                rows_head = slice(i * HEAD, (i + 1) * HEAD)
                probs = hidden[:, lanes((slot * 2 + i) * page_len, page_len)]
                delta = jnp.sum(jnp.where(of_head, weighted, 0.0), axis=1, keepdims=True)
                d_probs = jnp.dot(
                    jnp.where(of_head, d_o, jnp.zeros_like(d_o)),
                    v_t,
                    preferred_element_type=jnp.float32,
                )
                d_s = (probs.astype(jnp.float32) * (d_probs - delta)).astype(jnp.bfloat16)
                serve()
                d_b = jnp.dot(d_s, keys_k, preferred_element_type=jnp.float32)
                d_1, d_2 = d_b[:, : 2 * FREQ], d_b[:, 2 * FREQ : 4 * FREQ]
                cosine, sine = table[0], table[1]
                d_sine = (d_1 * sine - d_2 * cosine).astype(jnp.bfloat16)
                d_cosine = (d_1 * cosine + d_2 * sine).astype(jnp.bfloat16)
                d_u = jnp.concatenate([d_sine, d_cosine], axis=1)
                d_q = d_b[:, 4 * FREQ :] * (HEAD**-0.5) + jnp.dot(
                    d_u, w_t, preferred_element_type=jnp.float32
                )
                d_w = jnp.dot(q_t[rows_head], d_u, preferred_element_type=jnp.float32)
                box_g[pl.ds(pl.multiple_of(p * 128 + i * HEAD, HEAD), HEAD), :] = d_w.astype(
                    jnp.bfloat16
                )
                d_k = jnp.dot(q_t[rows_head], d_s, preferred_element_type=jnp.float32)
                d_v = jnp.dot(d_o_t[rows_head], probs, preferred_element_type=jnp.float32)
                grads.append((d_q, d_k * (HEAD**-0.5), d_v))
            (q_one, k_one, v_one), (q_two, k_two, v_two) = grads
            d_q = jnp.where(head_lane < HEAD, q_one, q_two).astype(jnp.bfloat16)
            d_k = jnp.concatenate([k_one, k_two], axis=0).astype(jnp.bfloat16).T
            d_v = jnp.concatenate([v_one, v_two], axis=0).astype(jnp.bfloat16).T
            for n, value in enumerate((d_q, d_k, d_v)):
                slope[:, lanes(n * width + p * 128, 128)] = value
            vec_g[:, lanes(BQ + p * 128, 128)] = total(d_q)
            vec_g[:, lanes(BV + p * 128, 128)] = total(d_v)
            return carry

        def qkv_grads(slot):
            store, top = ("early", 0) if slot == 0 else ("down", (slot - 1) * 48)
            for h in range(2):
                first = h * 1152 + THIRDS[h][slot] * 384
                tile = dot_n(x_own[...], slope[:, first : first + 384])
                stored[store][h, :, :, :, top : top + 48, :] = tile.astype(
                    jnp.bfloat16
                ).reshape(4, 2, 2, -1, 384)
            begin([g for g in range(count) if names[g] == "qkv"][slot])

        half = HEADS // 4
        clock.loop(half, pair, 4)
        qkv_grads(0)
        clock.point()
        clock.loop(half, lambda p, carry, serve: pair(p + half, carry, serve), 4)

        for dz in range(4):
            for dx in range(2):
                for dc in range(2):
                    for dy in range(2):
                        device = ((dz * 2 + dx) * 2 + dc) * 2 + dy
                        start = device * (VECTORS // 32) // 128 * 128
                        pieces[dy, dz, dx, dc] = vec_g[:, start : start + 384]
        vector_c.start()
        part = box_g[...]
        stored["box"][0] = jnp.concatenate(
            [part[:, :FREQ], part[:, 2 * FREQ : 3 * FREQ]], axis=1
        ).reshape(4, 2, 2, -1, 384)
        stored["box"][1] = jnp.concatenate(
            [part[:, FREQ : 2 * FREQ], part[:, 3 * FREQ :]], axis=1
        ).reshape(4, 2, 2, -1, 384)
        begin(names.index("box"))
        clock.point()
        clock.upto(*[
            (g, part, 3)
            for g, group in enumerate(groups)
            if names[g] == "down"
            for part in range(len(group[-1]))
        ])
        scatter.left([g for g in range(count) if names[g] == "down"], clock.at)

        for slot in (1, 2):
            qkv_grads(slot)
            clock.point()

        fetch_weight("qkv", w_qkv).wait()

        def back_tile(h, carry, serve):
            w = w_qkv.at[h][...].reshape(width, 1152)
            unit1[...] += dot_t(slope[:, lanes(h * 1152, 1152)], w)
            return carry

        clock.loop(2, back_tile)
        dx_low[0] = unit1[rows(1 - y), :].astype(jnp.bfloat16)
        dx_swap.start()
        pltpu.make_async_copy(unit1.at[rows(y)], dx_out.at[y], out_sem.at[1]).start()

        clock.point()
        clock.point()
        clock.upto(*(tuple(event) for _, *event in SCATTER_EVENTS))
        dx_swap.wait_recv()
        unit2[0:block, :] = dx_low[1].astype(jnp.float32)
        pltpu.make_async_copy(unit2.at[0:block], dx_out.at[1 - y], out_sem.at[2]).start()
        for k in range(3):
            vector_z(k).wait_recv()
        piece_total = pieces[y, z, x, c]
        for k in range(3):
            piece_total = piece_total + pz_land[k]
        piece_sum[...] = piece_total
        finals = [pltpu.make_async_copy(piece_sum, piece_out, out_sem.at[3])]
        for i, name in enumerate(WEIGHTS):
            finals.append(pltpu.make_async_copy(summed[name], grad_out[name], out_sem.at[4 + i]))
        for copy in finals:
            copy.start()
        scatter.left(range(count))
        for copy in (vector_c, vector_y, vector_x, out_swap, dx_swap):
            copy.wait_send()
        for k in range(3):
            vector_z(k).wait_send()
        out_swap.wait_recv()
        out_keep.wait()
        pltpu.make_async_copy(unit1.at[rows(y)], dx_out.at[y], out_sem.at[1]).wait()
        pltpu.make_async_copy(unit2.at[0:block], dx_out.at[1 - y], out_sem.at[2]).wait()
        for copy in finals:
            copy.wait()

    pl.run_scoped(
        with_qkv,
        pltpu.VMEM(w_in["qkv"].shape, jnp.bfloat16),
        pltpu.VMEM(stored["box"].shape, jnp.bfloat16),
    )


def backward_call(full, kept, shards):
    low, single = jnp.bfloat16, jnp.float32
    page_len, width = kept["x"].shape
    groups = SCATTER_GROUPS
    count = len(groups)
    outs = [
        jax.ShapeDtypeStruct((2, page_len // 2, width), low),
        jax.ShapeDtypeStruct((2, page_len // 2, width), single),
    ]
    outs += [jax.ShapeDtypeStruct(s.shape, single) for s in shards]
    outs += [jax.ShapeDtypeStruct((1, 384), single)]
    by_name = dict(zip(WEIGHTS, shards))

    def vmem(*shape, kind=low):
        return pltpu.VMEM(shape, kind)

    size = lambda cut: (cut[1], cut[3])
    dma = pltpu.SemaphoreType.DMA
    scratch = [vmem(2, 4, 2, 2, *by_name[n].shape) for n in ("box", "out", "up", "down")]
    scratch += [vmem(2, 4, 2, *size(g[2])) for g in groups]
    for group in groups:
        for path, piece in group[-1]:
            scratch += [vmem(*landing_shape(path, hop, piece)) for hop in range(3)]
    scratch += [vmem(*s.shape, kind=single) for s in shards]
    scratch += [vmem(*full[n].shape) for n in ("box", "out")]
    scratch += [vmem(width, BOX_DIM), vmem(width, BOX_DIM)]
    scratch += [vmem(*kept[n].shape, kind=kept[n].dtype) for n in ("ct", "qkv", "table")]
    scratch += [vmem(page_len, BOX_DIM)]
    scratch += [
        vmem(*kept[n].shape, kind=kept[n].dtype)
        for n in ("o", "unit1", "inv1", "g", "d", "unit2", "inv2", "vec")
    ]
    scratch += [vmem(page_len, width)] * 4
    scratch += [vmem(2, page_len // 2, width), vmem(1, VECTORS + 128, kind=single)]
    scratch += [
        vmem(2, 4, 2, 2, 1, 384, kind=single),
        vmem(2, 4, 2, 1, 384, kind=single),
        vmem(4, 2, 1, 384, kind=single),
        vmem(4, 1, 384, kind=single),
        vmem(3, 1, 384, kind=single),
        vmem(1, 384, kind=single),
    ]
    scratch += [dma((SENDS,)), dma((len(semaphore_table(groups, 4)),))] + [dma((count,))] * 2
    scratch += [dma((3,))] * 2 + [dma((3,))] * 2 + [dma((2,))] * 2
    scratch += [dma((17,)), dma((2, 2)), dma((9,))]
    anywhere = pl.BlockSpec(memory_space=pl.ANY)
    operands = [full[n] for n in WEIGHTS] + list(kept.values())
    plan = (groups, page_len, width)
    results = pl.pallas_call(
        partial(backward_kernel, plan),
        out_shape=outs,
        in_specs=[anywhere] * len(operands),
        out_specs=[anywhere] * len(outs),
        scratch_shapes=scratch,
        compiler_params=pltpu.CompilerParams(
            collective_id=1, has_side_effects=True, vmem_limit_bytes=VMEM_BACK
        ),
    )(*operands)
    return results


VMEM_BACK = 63 * 2**20


def finish_kernel(*refs):
    count = len(refs) // 2
    ins, outs = refs[:count], refs[count:]
    for i in range(count - 1):
        outs[i][...] = ins[i][...]
    rows = jnp.broadcast_to(ins[-1][...], (8, 384))
    rows = pltpu.roll(rows, 384 - Place().vector_offset(), 1)
    outs[-1][...] = rows[0:1, : VECTORS // 32].reshape(VECTORS // 32)


def finish_call(results):
    outs = [jax.ShapeDtypeStruct(r.shape, r.dtype) for r in results[:-1]]
    outs += [jax.ShapeDtypeStruct((VECTORS // 32,), jnp.float32)]

    def half(shape):
        block = (shape[0] // 2,) + shape[1:]
        return pl.BlockSpec(block, lambda i: (i,) + (0,) * (len(shape) - 1))

    halves = [half(r.shape) for r in results[:-1]]
    return pl.pallas_call(
        finish_kernel,
        out_shape=outs,
        grid=(2,),
        in_specs=halves + [pl.BlockSpec((1, 384), lambda i: (0, 0))],
        out_specs=halves + [pl.BlockSpec((VECTORS // 32,), lambda i: (0,))],
        compiler_params=pltpu.CompilerParams(vmem_limit_bytes=VMEM_BACK),
    )(*results)


def fast_layer(tokens, boxes, lengths, wqkv, wbox, wout, wup, wdown, vectors, cotangent):
    shards = (wqkv, wbox, wout, wup, wdown)
    full, kept = forward_call(tokens, cotangent, boxes, lengths, vectors, shards)
    return tuple(finish_call(backward_call(full, kept, shards)))


def on_device(*args):
    tokens, wqkv, wbox, wdown = args[0], args[3], args[4], args[7]
    blocks, groups = lax.axis_size("blk"), lax.axis_size("dp")
    fits = (
        blocks == 2
        and groups == 16
        and tokens.shape[0] == 2
        and wqkv.shape == (48, 1152)
        and wdown.shape == (192, 384)
        and wbox.shape == (48, 2 * FREQ)
    )
    return fast_layer(*args) if fits else general_layer(*args)


def solution(mesh):
    in_specs = (
        P("dp", "blk", None),
        P(None, "dp", "blk"),
        P("dp"),
        P("dp", "blk"),
        P("dp", "blk"),
        P("dp", "blk"),
        P("dp", "blk"),
        P("dp", "blk"),
        P(("dp", "blk")),
        P("dp", "blk", None),
    )
    out_specs = (
        P("dp", "blk", None),
        P("dp", "blk", None),
        P("dp", "blk"),
        P("dp", "blk"),
        P("dp", "blk"),
        P("dp", "blk"),
        P("dp", "blk"),
        P(("dp", "blk")),
    )
    return jax.shard_map(
        on_device, mesh=mesh, in_specs=in_specs, out_specs=out_specs, check_vma=False
    )
```

profile of v0, /device:TPU:0, one launch (start us, length us, event | category | flops | bytes accessed | tf_op | source)
XLA Modules:
  0.0 169.1 jit_solution(12846421065007427015)
XLA Ops:
  0.6 83.5 %shard_map.161 = (bf16[2,4,2,2,48,1152]{5,4,3,2,1,0:T(8,128)(2,1)}, bf16[2,4,2,2,48,384]{5,4,3,2,1,0:T(8,128)(2,1)}, bf16[2,4,2,2,48,384]{5,4,3,2,1,0:T(8,128)(2...) custom-call(bf16[2,256,768]{2,1,0:T(8,128)(2,1)} %refs_0_.1, ...), custom_call_target="tpu_custom_call" | custom-call | tf_op jit(solution)/shard_map/pallas_call | solution.py:1143
  84.2 81.3 %shard_map.162 = (bf16[2,256,768]{2,1,0:T(8,128)(2,1)}, f32[2,256,768]{2,1,0:T(8,128)}, f32[48,1152]{1,0:T(8,128)}, f32[48,384]{1,0:T(8,128)}, f32[48,384]{1,0:T...) custom-call(bf16[2,4,2,2,48,1152]{5,4,3,2,1,0:T(8,128)(2,1)} %get-tuple-element.34.refs_0_, ...), custom_call_target="tpu_custom_call" | custom-call | tf_op jit(solution)/shard_map/pallas_call | solution.py:1787
  165.5 3.4 %shard_map.163 = (bf16[2,256,768]{2,1,0:T(8,128)(2,1)}, f32[2,256,768]{2,1,0:T(8,128)}, f32[48,1152]{1,0:T(8,128)}, f32[48,384]{1,0:T(8,128)}, f32[48,384]{1,0:T...) custom-call(bf16[2,256,768]{2,1,0:T(8,128)(2,1)} %get-tuple-element.52.refs_0_, ...), custom_call_target="tpu_custom_call" | custom-call | tf_op jit(solution)/shard_map/pallas_call | solution.py:1822
where the time goes:
time: 169 us
  Pallas kernels  168 us (99%)
    pallas_call x1, Pallas kernels, forward_call(): pl.pallas_call(partial(forward_kernel, plan), out_shape=outs, in_specs=[a...  83.5 us
    pallas_call x1, Pallas kernels, backward_call(): pl.pallas_call(partial(backward_kernel, plan), out_shape=outs, in_specs=[...  81.3 us
    pallas_call x1, Pallas kernels, finish_call(): pl.pallas_call(finish_kernel, out_shape=outs, grid=(2,), in_specs=halves...  3.4 us

commit v1 on v0

--- a/solution.py
+++ b/solution.py
@@ -198,242 +198,243 @@
 
 GATHER_GROUPS = (
     ("qkv", (0, 48, 0, 384), (("zxy", (0, 48, 0, 384)),)),
-    ("qkv", (0, 48, 384, 384), (("yzx", (0, 48, 384, 256)), ("yzx", (0, 48, 640, 128)),)),
+    ("qkv", (0, 48, 384, 384), (("zyx", (0, 48, 384, 256)), ("yzx", (0, 48, 640, 128)),)),
     ("qkv", (0, 48, 768, 384), (("zxy", (0, 48, 768, 384)),)),
-    ("box", (0, 48, 0, 384), (("zxy", (0, 48, 0, 256)), ("yzx", (0, 48, 256, 128)),)),
-    ("out", (0, 48, 0, 384), (("yxz", (0, 48, 0, 128)), ("xzy", (0, 48, 128, 256)),)),
-    ("up", (0, 48, 0, 384), (("yxz", (0, 48, 0, 256)), ("zyx", (0, 48, 256, 128)),)),
-    ("up", (0, 48, 384, 384), (("zyx", (0, 48, 384, 384)),)),
+    ("box", (0, 48, 0, 384), (("zyx", (0, 48, 0, 256)), ("yzx", (0, 48, 256, 128)),)),
+    ("out", (0, 48, 0, 384), (("zxy", (0, 48, 0, 256)), ("yxz", (0, 48, 256, 128)),)),
+    ("up", (0, 48, 0, 384), (("zxy", (0, 48, 0, 256)), ("yzx", (0, 48, 256, 128)),)),
+    ("up", (0, 48, 384, 384), (("yxz", (0, 48, 384, 384)),)),
     ("up", (0, 48, 768, 384), (("yxz", (0, 48, 768, 384)),)),
-    ("up", (0, 48, 1152, 384), (("zyx", (0, 48, 1152, 256)), ("zyx", (0, 48, 1408, 128)),)),
+    ("up", (0, 48, 1152, 384), (("zxy", (0, 48, 1152, 256)), ("zyx", (0, 48, 1408, 128)),)),
     ("down", (0, 192, 0, 128), (("zxy", (0, 64, 0, 128)), ("yxz", (64, 128, 0, 128)),)),
-    ("down", (0, 192, 128, 128), (("zyx", (0, 64, 128, 128)), ("xzy", (64, 128, 128, 128)),)),
-    ("down", (0, 192, 256, 128), (("zxy", (0, 192, 256, 128)),)),
+    ("down", (0, 192, 128, 128), (("zxy", (0, 128, 128, 128)), ("yzx", (128, 64, 128, 128)),)),
+    ("down", (0, 192, 256, 128), (("zyx", (0, 192, 256, 128)),)),
 )
 GATHER_EVENTS = (
     (1, 0, 0, 0),
-    (1, 1, 1, 0),
+    (1, 1, 0, 0),
     (1, 2, 0, 0),
     (1, 3, 0, 0),
+    (1, 4, 1, 0),
     (1, 0, 0, 10),
+    (1, 1, 0, 10),
     (1, 0, 0, 1),
+    (1, 8, 0, 0),
     (1, 6, 0, 0),
+    (1, 10, 1, 0),
     (1, 3, 1, 0),
-    (1, 5, 0, 0),
-    (1, 8, 1, 0),
+    (1, 5, 1, 0),
+    (1, 1, 1, 0),
     (1, 2, 0, 10),
-    (1, 4, 0, 0),
-    (1, 1, 0, 0),
-    (2, 9, 0, 0),
+    (1, 1, 0, 1),
+    (1, 10, 0, 0),
     (2, 3, 0, 10),
     (2, 7, 0, 0),
     (2, 2, 0, 1),
-    (2, 9, 1, 0),
-    (2, 1, 1, 1),
-    (2, 8, 0, 0),
-    (2, 0, 0, 2),
-    (3, 1, 0, 1),
-    (3, 3, 0, 1),
-    (4, 7, 0, 1),
-    (4, 1, 1, 11),
-    (4, 3, 1, 1),
-    (4, 4, 0, 1),
-    (4, 2, 0, 2),
-    (4, 9, 0, 10),
-    (5, 5, 1, 0),
-    (5, 10, 1, 0),
-    (6, 4, 1, 0),
-    (7, 1, 1, 2),
-    (7, 6, 0, 10),
-    (7, 1, 0, 11),
-    (8, 3, 0, 2),
-    (8, 9, 0, 1),
-    (8, 3, 1, 11),
-    (8, 11, 0, 0),
-    (8, 10, 1, 1),
-    (9, 8, 0, 10),
-    (9, 8, 1, 10),
-    (9, 1, 0, 2),
-    (9, 6, 0, 1),
-    (10, 0, 0, 3),
+    (3, 4, 0, 0),
+    (3, 1, 1, 1),
+    (3, 0, 0, 2),
+    (3, 4, 1, 1),
+    (3, 3, 1, 1),
+    (4, 6, 0, 1),
+    (4, 4, 0, 10),
+    (4, 1, 0, 2),
+    (5, 3, 0, 1),
+    (5, 5, 0, 0),
+    (5, 5, 1, 1),
+    (5, 10, 1, 1),
+    (6, 1, 1, 11),
+    (6, 5, 0, 10),
+    (6, 2, 0, 2),
+    (7, 4, 0, 1),
+    (7, 8, 0, 10),
+    (7, 9, 0, 0),
+    (7, 9, 1, 0),
+    (7, 5, 1, 11),
+    (7, 3, 1, 11),
+    (8, 1, 1, 2),
+    (8, 8, 1, 0),
+    (8, 0, 0, 3),
+    (9, 9, 0, 10),
+    (9, 7, 0, 1),
+    (9, 3, 0, 2),
+    (9, 3, 1, 2),
+    (10, 11, 0, 0),
+    (10, 0, 0, 4),
+    (10, 4, 1, 2),
+    (10, 1, 0, 3),
+    (10, 8, 1, 10),
+    (10, 9, 0, 1),
+    (10, 4, 0, 2),
     (10, 1, 1, 3),
-    (10, 0, 0, 4),
-    (11, 5, 1, 10),
-    (12, 10, 0, 0),
-    (12, 3, 1, 2),
+    (10, 10, 1, 11),
+    (11, 10, 0, 10),
+    (11, 1, 0, 4),
+    (11, 11, 0, 10),
     (12, 2, 0, 3),
-    (12, 9, 1, 1),
+    (12, 6, 0, 2),
+    (12, 1, 1, 4),
+    (12, 2, 0, 4),
+    (12, 10, 0, 1),
     (13, 5, 0, 1),
-    (13, 11, 0, 10),
-    (13, 10, 1, 11),
-    (13, 4, 1, 1),
-    (13, 8, 0, 1),
-    (14, 1, 0, 3),
-    (14, 4, 0, 2),
-    (15, 5, 1, 1),
-    (16, 8, 1, 1),
-    (18, 1, 1, 4),
-    (18, 2, 0, 4),
-    (18, 9, 0, 2),
-    (18, 1, 0, 4),
-    (18, 11, 0, 1),
-    (20, 3, 1, 3),
-    (20, 10, 1, 2),
-    (21, 3, 0, 3),
-    (21, 4, 1, 11),
-    (21, 5, 0, 2),
-    (21, 7, 0, 2),
-    (22, 10, 0, 10),
-    (22, 3, 1, 4),
-    (22, 9, 1, 2),
-    (22, 6, 0, 2),
-    (23, 3, 0, 4),
-    (23, 8, 0, 2),
-    (26, 4, 0, 12),
-    (27, 5, 1, 2),
-    (27, 10, 0, 1),
-    (28, 4, 1, 2),
-    (31, 11, 0, 2),
-    (32, 10, 0, 2),
-    (32, 5, 0, 12),
-    (33, 7, 0, 12),
-    (33, 4, 0, 3),
-    (34, 6, 0, 3),
-    (35, 9, 0, 3),
-    (36, 8, 1, 2),
-    (37, 4, 1, 3),
-    (39, 10, 1, 3),
-    (42, 8, 0, 3),
-    (44, 6, 0, 4),
-    (46, 5, 1, 3),
-    (46, 9, 0, 4),
-    (49, 4, 0, 4),
-    (54, 10, 0, 3),
-    (55, 5, 0, 3),
-    (56, 4, 1, 4),
-    (56, 7, 0, 3),
-    (57, 10, 1, 4),
-    (61, 5, 1, 4),
-    (62, 8, 1, 3),
-    (63, 10, 0, 4),
-    (64, 9, 1, 12),
-    (79, -1, 0, 0),
-    (80, 5, 0, 4),
-    (81, 11, 0, 3),
-    (93, 7, 0, 4),
-    (93, 8, 1, 4),
-    (95, 9, 1, 3),
-    (102, 8, 0, 4),
-    (124, 9, 1, 4),
-    (131, 11, 0, 4),
+    (13, 8, 1, 1),
+    (13, 3, 0, 3),
+    (14, 5, 1, 2),
+    (14, 8, 0, 1),
+    (14, 7, 0, 2),
+    (14, 10, 1, 2),
+    (15, 3, 1, 3),
+    (16, 9, 1, 1),
+    (16, 11, 0, 1),
+    (16, 4, 0, 3),
+    (16, 3, 0, 4),
+    (17, 9, 0, 2),
+    (19, 3, 1, 4),
+    (20, 5, 0, 2),
+    (20, 4, 1, 12),
+    (22, 6, 0, 12),
+    (26, 8, 0, 2),
+    (26, 8, 1, 2),
+    (26, 4, 1, 3),
+    (27, 4, 0, 4),
+    (27, 5, 1, 3),
+    (28, 11, 0, 2),
+    (28, 10, 0, 2),
+    (29, 10, 1, 3),
+    (29, 7, 0, 12),
+    (29, 9, 1, 2),
+    (32, 5, 0, 3),
+    (32, 6, 0, 3),
+    (34, 9, 0, 3),
+    (34, -1, 0, 0),
+    (35, 4, 1, 4),
+    (37, 8, 1, 3),
+    (39, 9, 1, 12),
+    (46, 7, 0, 3),
+    (47, 10, 0, 3),
+    (51, 8, 0, 3),
+    (54, 5, 0, 4),
+    (54, 9, 0, 4),
+    (55, 6, 0, 4),
+    (56, 11, 0, 3),
+    (67, 5, 1, 4),
+    (71, 7, 0, 4),
+    (71, 9, 1, 3),
+    (75, 10, 1, 4),
+    (78, 11, 0, 4),
+    (82, 8, 0, 4),
+    (87, 8, 1, 4),
+    (88, 9, 1, 4),
+    (111, 10, 0, 4),
 )
 SCATTER_GROUPS = (
-    ("down", "down", (0, 192, 0, 128), (0, 192, 0, 128), (("zxy", (0, 64, 0, 128)), ("xzy", (64, 128, 0, 128)),)),
+    ("down", "down", (0, 192, 0, 128), (0, 192, 0, 128), (("zyx", (0, 64, 0, 128)), ("xzy", (64, 128, 0, 128)),)),
     ("down", "down", (0, 192, 128, 128), (0, 192, 128, 128), (("zxy", (0, 64, 128, 128)), ("yxz", (64, 128, 128, 128)),)),
     ("down", "down", (0, 192, 256, 128), (0, 192, 256, 128), (("yzx", (0, 192, 256, 128)),)),
     ("up", "up", (0, 48, 0, 384), (0, 48, 0, 384), (("xyz", (0, 48, 0, 128)), ("yxz", (0, 48, 128, 256)),)),
     ("up", "up", (0, 48, 384, 384), (0, 48, 384, 384), (("xyz", (0, 48, 384, 384)),)),
     ("up", "up", (0, 48, 768, 384), (0, 48, 768, 384), (("xyz", (0, 48, 768, 384)),)),
     ("up", "up", (0, 48, 1152, 384), (0, 48, 1152, 384), (("xyz", (0, 48, 1152, 384)),)),
-    ("out", "out", (0, 48, 0, 384), (0, 48, 0, 384), (("zyx", (0, 48, 0, 256)), ("yxz", (0, 48, 256, 128)),)),
+    ("out", "out", (0, 48, 0, 384), (0, 48, 0, 384), (("zxy", (0, 48, 0, 256)), ("xyz", (0, 48, 256, 128)),)),
     ("qkv", "early", (0, 48, 0, 384), 0, (("zxy", (0, 48, 0, 384)),)),
     ("box", "box", (0, 48, 0, 384), (0, 48, 0, 384), (("yxz", (0, 48, 0, 128)), ("xyz", (0, 48, 128, 256)),)),
     ("qkv", "down", (0, 48, 0, 384), 1, (("yxz", (0, 48, 0, 128)), ("yxz", (0, 48, 128, 256)),)),
     ("qkv", "down", (48, 48, 0, 384), 2, (("yxz", (48, 48, 0, 128)), ("xzy", (48, 48, 128, 256)),)),
 )
 SCATTER_EVENTS = (
-    (4, 0, 0, 0),
+    (5, 0, 0, 0),
     (6, 1, 0, 0),
+    (11, 2, 0, 0),
     (12, 0, 0, 10),
-    (12, 2, 0, 0),
-    (15, 0, 1, 1),
-    (15, 5, 0, 0),
+    (13, 3, 0, 0),
+    (13, 4, 0, 0),
+    (16, 0, 1, 1),
     (16, 1, 0, 10),
-    (17, 0, 1, 11),
-    (17, 4, 0, 0),
-    (18, 3, 0, 0),
-    (19, 7, 0, 0),
-    (19, -1, 0, 0),
-    (22, 1, 0, 1),
-    (24, 0, 0, 1),
-    (24, 2, 0, 1),
-    (24, 7, 0, 10),
+    (17, 0, 0, 1),
+    (17, 5, 0, 0),
+    (18, 7, 0, 0),
+    (21, 0, 1, 11),
+    (25, 2, 0, 1),
     (25, 1, 1, 1),
-    (27, 4, 0, 1),
-    (31, 6, 0, 0),
-    (32, 3, 1, 1),
-    (32, 2, 0, 11),
+    (25, -1, 0, 0),
+    (26, 7, 0, 10),
+    (28, 1, 0, 1),
+    (29, 6, 0, 0),
+    (30, 3, 1, 1),
+    (31, 4, 0, 1),
+    (31, 2, 0, 11),
+    (32, 0, 0, 2),
+    (32, 5, 0, 1),
     (34, 1, 1, 2),
-    (35, 8, 0, 0),
+    (34, 8, 0, 0),
+    (35, 0, 1, 2),
     (35, 1, 0, 2),
-    (36, 5, 0, 1),
-    (38, 0, 1, 2),
-    (39, 1, 1, 12),
-    (41, 0, 0, 2),
-    (41, 6, 0, 1),
-    (41, 2, 0, 2),
-    (45, 4, 0, 2),
-    (45, 0, 1, 3),
-    (46, 1, 1, 3),
-    (46, 8, 0, 10),
-    (46, 3, 0, 1),
-    (47, 7, 0, 1),
-    (47, 9, 0, 0),
+    (36, 1, 1, 12),
+    (42, 2, 0, 2),
+    (42, 6, 0, 1),
+    (43, 8, 0, 10),
+    (44, 1, 1, 3),
+    (45, 3, 0, 1),
+    (46, 2, 0, 3),
+    (46, 4, 0, 2),
     (47, 1, 0, 3),
-    (47, 0, 0, 3),
-    (47, 2, 0, 3),
-    (48, 3, 1, 2),
+    (47, 7, 1, 1),
+    (48, 0, 0, 3),
+    (48, 9, 0, 0),
+    (48, 0, 1, 3),
     (48, -2, 0, 0),
-    (48, 7, 1, 1),
-    (48, 10, 0, 0),
-    (49, 4, 0, 12),
-    (49, 6, 0, 2),
+    (48, 6, 0, 2),
+    (49, 10, 0, 0),
+    (49, 7, 1, 2),
     (49, 11, 0, 0),
-    (50, 9, 1, 1),
-    (51, 3, 0, 2),
-    (62, 5, 0, 2),
+    (49, 3, 1, 2),
+    (51, 9, 1, 1),
+    (51, 7, 0, 1),
+    (57, 3, 0, 2),
     (64, 9, 0, 1),
-    (67, -2, 0, 1),
-    (68, 7, 0, 2),
-    (71, 3, 0, 12),
-    (78, 7, 1, 2),
-    (89, 11, 1, 1),
-    (98, 10, 1, 1),
-    (100, 4, 0, 3),
-    (117, -2, 0, 2),
-    (128, 3, 0, 3),
-    (183, 8, 0, 1),
-    (521, 6, 0, 12),
-    (525, 3, 1, 12),
-    (544, 11, 1, 11),
-    (563, 5, 0, 12),
-    (615, 7, 1, 12),
-    (874, 10, 0, 1),
-    (912, 9, 0, 2),
-    (918, 9, 1, 2),
-    (959, 11, 0, 1),
+    (65, 4, 0, 12),
+    (65, 3, 0, 12),
+    (68, -2, 0, 1),
+    (75, 5, 0, 2),
+    (75, 11, 1, 1),
+    (81, 10, 1, 1),
+    (88, 7, 0, 2),
+    (95, -2, 0, 2),
+    (117, 4, 0, 3),
+    (146, 3, 0, 3),
+    (198, 8, 0, 1),
+    (530, 3, 1, 12),
+    (543, 6, 0, 12),
+    (567, 5, 0, 12),
+    (567, 11, 1, 11),
+    (568, 7, 1, 12),
+    (898, 10, 0, 1),
+    (912, 9, 1, 2),
+    (915, 9, 0, 2),
+    (936, 11, 0, 1),
+    (956, 8, 0, 2),
     (959, 10, 0, 2),
     (975, 9, 1, 12),
-    (978, 11, 0, 2),
-    (979, 10, 1, 2),
-    (979, 8, 0, 2),
-    (999, 10, 0, 12),
-    (1000, 11, 1, 2),
-    (1002, 9, 0, 12),
-    (1010, 3, 1, 3),
-    (1020, 11, 0, 12),
-    (1021, 9, 1, 3),
-    (1032, 10, 0, 3),
-    (1049, 10, 1, 12),
-    (1059, 5, 0, 3),
-    (1066, 11, 0, 3),
-    (1068, 8, 0, 3),
-    (1070, 7, 0, 3),
-    (1073, 6, 0, 3),
+    (988, 11, 0, 2),
+    (991, 10, 0, 12),
+    (1004, 10, 1, 2),
+    (1005, 9, 0, 12),
+    (1009, 11, 1, 2),
+    (1017, 9, 1, 3),
+    (1019, 11, 0, 12),
+    (1022, 3, 1, 3),
+    (1030, 10, 0, 3),
+    (1046, 6, 0, 3),
+    (1054, 10, 1, 12),
+    (1058, 5, 0, 3),
+    (1068, 7, 0, 3),
+    (1069, 11, 0, 3),
+    (1069, -2, 0, 3),
+    (1070, 8, 0, 3),
     (1084, 9, 0, 3),
-    (1095, 10, 1, 3),
-    (1123, 11, 1, 3),
-    (1148, 7, 1, 3),
+    (1086, 10, 1, 3),
+    (1111, 11, 1, 3),
+    (1136, 7, 1, 3),
 )
 
 
@@ -473,13 +474,16 @@
         device = ((self.z * 2 + self.x) * 2 + self.c) * 2 + self.y
         return lax.rem(device * (VECTORS // 32), 128)
 
-    def greet(self):
-        barrier = pltpu.get_barrier_semaphore()
+    def hail(self):
         peers = [self.near_peer, self.far_peer, self.mirror_peer]
         peers += [self.x_peer, self.y_peer, self.c_peer]
         for peer in peers:
-            pl.semaphore_signal(barrier, inc=1, device_id=peer, device_id_type=MESH)
-        pl.semaphore_wait(barrier, len(peers))
+            pl.semaphore_signal(
+                pltpu.get_barrier_semaphore(), inc=1, device_id=peer, device_id_type=MESH
+            )
+
+    def meet(self):
+        pl.semaphore_wait(pltpu.get_barrier_semaphore(), 6)
 
 
 def semaphore_table(groups, slots):
@@ -763,6 +767,18 @@
 
 BQ, BV, BO, G1, E1, B1, B2, G2, E2 = 0, 768, 1536, 2304, 3072, 3840, 6912, 7680, 8448
 VECTORS = 9216
+SUMS = VECTORS + 128
+
+
+def total(value):
+    return jnp.sum(value.astype(jnp.float32), axis=0, keepdims=True)
+
+
+def norm_back(grad, unit, inverse, gain):
+    scaled = grad * gain
+    mean_grad = jnp.mean(scaled, axis=1, keepdims=True)
+    mean_unit = jnp.mean(scaled * unit, axis=1, keepdims=True)
+    return inverse * (scaled - mean_grad - unit * mean_unit)
 
 
 def forward_kernel(plan, *refs):
@@ -774,10 +790,10 @@
     shards = dict(zip(WEIGHTS, take(5)))
     full_out = dict(zip(WEIGHTS, take(5)))
     (x_out, ct_out, qkv_out, table_out, p_out, o_out, unit1_out, inv1_out) = take(8)
-    (g_out, d_out, unit2_out, inv2_out, vec_out) = take(5)
+    (g_out, d_out, unit2_out, low_out, vec_out) = take(5)
     full = dict(zip(WEIGHTS, take(5)))
-    (x_own, boxes_peer, pieces, vec, qkv, table, keys, box_w, p_slots, o_own, o_low) = take(11)
-    (unit1, inv1, y1_low, hidden, slope, unit2, inv2) = take(7)
+    (ct_own, x_own, boxes_peer, pieces, vec, qkv, table, keys, box_w, p_slots, o_own, o_low) = take(12)
+    (unit1, inv1, y1_low, hidden, slope, unit2) = take(6)
     w_sems = take(2)
     (own_sem,) = take(1)
     vz_sems, vxy_sems, vc_sems = take(2), take(2), take(2)
@@ -825,7 +841,7 @@
 
     def event(g, part, step):
         if g < 0:
-            swap(1, cotangent, ct_out).start()
+            swap(1, cotangent, ct_own).start()
         else:
             gather.step(g, part, step)
 
@@ -841,21 +857,22 @@
         copy.start()
         outgoing.append(copy)
 
+    place.hail()
+    gather.own()
     own_vector = vectors[...].astype(jnp.float32).reshape(1, -1)
     own_vector = jnp.concatenate(
         [own_vector, jnp.zeros((1, 384 - own_vector.shape[1]), jnp.float32)], axis=1
     )
     own_vector = jnp.broadcast_to(own_vector, (8, 384))
     piece[...] = pltpu.roll(own_vector, place.vector_offset(), 1)[0:1, :]
-    place.greet()
-    gather.own()
+    place.meet()
     box_swap.start()
     vector_y().start()
     vector_own.start()
     swap(0, tokens, x_own).start()
     clock.point()
     keep(0, tokens, x_own).start()
-    keep(1, cotangent, ct_out).start()
+    keep(1, cotangent, ct_own).start()
 
     box_swap.wait_recv()
     mine, other = boxes[...], boxes_peer[...]
@@ -899,22 +916,25 @@
                     device = ((dz * 2 + dx) * 2 + dc) * 2 + dy
                     start = device * (VECTORS // 32) // 128 * 128
                     vec[:, start : start + 384] += pieces[dy, dz, dx, dc]
-    send_out(vec, vec_out)
 
     def vector(start, size=width):
         return vec[:, start : start + size]
 
+    def columns_of(name, first, count):
+        halves = [
+            full[name].at[h][:, :, :, :, first : first + count].reshape(-1, count)
+            for h in range(2)
+        ]
+        return jnp.concatenate(halves, axis=1)
+
     def project(first, count):
-        def project_tile(h, carry):
-            w = full["qkv"].at[h][:, :, :, :, first : first + count].reshape(width, count)
-            out = jnp.dot(x_own[...], w, preferred_element_type=jnp.float32)
-            start = pl.multiple_of(h * 1152 + first, 128)
-            column = start + lax.broadcasted_iota(jnp.int32, (1, count), 1)
-            bias = bias_qkv[:, lanes(start, count)]
-            qkv[:, lanes(start, count)] = (out + bias).astype(jnp.bfloat16)
-            return carry
-
-        lax.fori_loop(0, 2, project_tile, 0)
+        both = jnp.dot(
+            x_own[...], columns_of("qkv", first, count), preferred_element_type=jnp.float32
+        )
+        for h in range(2):
+            at = slice(h * 1152 + first, h * 1152 + first + count)
+            part = both[:, h * count : (h + 1) * count]
+            qkv[:, at] = (part + bias_qkv[:, at]).astype(jnp.bfloat16)
 
     bias_qkv[:, 0:width] = vector(BQ)
     bias_qkv[:, width : 2 * width] = jnp.zeros((1, width), jnp.float32)
@@ -1052,20 +1072,29 @@
             columns = (ALL,) * 4 + window(cut)
             send_out(full["down"].at[columns], full_out["down"].at[columns])
 
-            def down_body(h, carry, first=first, count=count):
-                w = full["down"].at[h][:, :, :, :, first : first + count].reshape(4 * width, count)
-                at = lanes(h * 384 + first, count)
-                unit2[:, at] += jnp.dot(hidden[...], w, preferred_element_type=jnp.float32)
-                return carry
-
-            lax.fori_loop(0, 2, down_body, 0)
+            both = jnp.dot(
+                hidden[...], columns_of("down", first, count), preferred_element_type=jnp.float32
+            )
+            for h in range(2):
+                at = slice(h * 384 + first, h * 384 + first + count)
+                unit2[:, at] += both[:, h * count : (h + 1) * count]
             clock.point()
     clock.upto(*(tuple(event) for _, *event in GATHER_EVENTS))
+    swap(1, cotangent, ct_own, True).wait_recv()
+    keep(1, cotangent, ct_own).wait()
     unit, inverse = norm(unit2[...])
-    unit2[...] = unit
-    inv2[...] = jnp.broadcast_to(inverse, (page_len, 128))
+    y1_low[...] = (unit * vector(G2) + vector(E2)).astype(jnp.bfloat16)
+    send_out(y1_low, low_out)
+    seed = ct_own[...].astype(jnp.float32)
+    d_h2 = norm_back(seed, unit, inverse, vector(G2))
+    unit2[...] = d_h2
     send_out(unit2, unit2_out)
-    send_out(inv2, inv2_out)
+    d_f = d_h2.astype(jnp.bfloat16)
+    ct_own[...] = d_f
+    send_out(ct_own, ct_out)
+    for n, value in enumerate((d_f, seed * unit, seed)):
+        vec[:, SUMS + n * width : SUMS + (n + 1) * width] = total(value)
+    send_out(vec, vec_out)
 
     gather.sends.left(gather.copy)
     for k in range(1, 4):
@@ -1075,9 +1104,7 @@
     vector_c().wait_send()
     box_swap.wait_send()
     swap(0, tokens, x_own).wait_send()
-    swap(1, cotangent, ct_out).wait_send()
-    swap(1, cotangent, ct_out, True).wait_recv()
-    keep(1, cotangent, ct_out).wait()
+    swap(1, cotangent, ct_own).wait_send()
     for copy in outgoing:
         copy.wait()
 
@@ -1104,8 +1131,8 @@
         g=((page_len, 4 * width), low),
         d=((page_len, 4 * width), low),
         unit2=((page_len, width), single),
-        inv2=((page_len, 128), single),
-        vec=((1, VECTORS + 128), single),
+        low=((page_len, width), low),
+        vec=((1, SUMS + 3 * width), single),
     )
     outs = full + [jax.ShapeDtypeStruct(*kinds[k]) for k in kinds]
     anywhere = pl.BlockSpec(memory_space=pl.ANY)
@@ -1115,9 +1142,10 @@
     scratch = [pltpu.VMEM(f.shape, f.dtype) for f in full]
     scratch += [
         pltpu.VMEM((page_len, width), low),
+        pltpu.VMEM((page_len, width), low),
         pltpu.VMEM(boxes.shape, jnp.int32),
         pltpu.VMEM((2, 4, 2, 2, 1, 384), single),
-        pltpu.VMEM((1, VECTORS + 128), single),
+        pltpu.VMEM((1, SUMS + 3 * width), single),
         pltpu.VMEM((page_len, 3 * width), low),
         pltpu.VMEM((2, page_len, 2 * FREQ), single),
         pltpu.VMEM((BOX_DIM, page_len), low),
@@ -1131,7 +1159,6 @@
         pltpu.VMEM((page_len, 4 * width), low),
         pltpu.VMEM((page_len, 4 * width), low),
         pltpu.VMEM((page_len, width), single),
-        pltpu.VMEM((page_len, 128), single),
     ]
     arrivals = len(semaphore_table(groups, 3)) + len(core_table(groups))
     scratch += [dma((SENDS,)), dma((arrivals,))]
@@ -1340,7 +1367,7 @@
     take = lambda n: [next(refs) for _ in range(n)]
     w_in = dict(zip(WEIGHTS, take(5)))
     (x_in, ct_in, qkv_in, table_in, p_in, o_in, unit1_in, inv1_in) = take(8)
-    (g_in, d_in, unit2_in, inv2_in, vec_in) = take(5)
+    (g_in, d_in, unit2_in, low_in, vec_in) = take(5)
     out_out, dx_out = take(2)
     grad_out = dict(zip(WEIGHTS, take(5)))
     (piece_out,) = take(1)
@@ -1350,8 +1377,8 @@
     landing = [[take(3) for _ in group[-1]] for group in groups]
     summed = dict(zip(WEIGHTS, take(5)))
     w_box, w_out, box_w, box_g = take(4)
-    (ct, qkv, table, keys, o_own, unit1, inv1, hidden, slope, unit2, inv2, vec) = take(12)
-    (y1_low, d_a, d_mixed, out_low, dx_low, vec_g) = take(6)
+    (ct, qkv, table, keys, o_own, unit1, inv1, hidden, slope, unit2, out_low, vec) = take(12)
+    (y1_low, d_a, d_mixed, dx_low, vec_g) = take(5)
     pieces, pc_land, py_land, px_land, pz_land, piece_sum = take(6)
     w_sems, c_sems = take(2), take(2)
     v_sems, vz_sems, ex_sems = take(2), take(2), take(2)
@@ -1364,7 +1391,7 @@
     sources = dict(
         unit2=(unit2_in, unit2),
         ct=(ct_in, ct),
-        inv2=(inv2_in, inv2),
+        low=(low_in, out_low),
         vec=(vec_in, vec),
         g=(g_in, hidden),
         d=(d_in, slope),
@@ -1390,24 +1417,33 @@
     def vector(start, size=width):
         return vec[:, start : start + size]
 
-    def total(value):
-        return jnp.sum(value.astype(jnp.float32), axis=0, keepdims=True)
-
-    def norm_back(grad, unit, inverse, gain):
-        scaled = grad * gain
-        mean_grad = jnp.mean(scaled, axis=1, keepdims=True)
-        mean_unit = jnp.mean(scaled * unit, axis=1, keepdims=True)
-        return inverse * (scaled - mean_grad - unit * mean_unit)
-
     names = [group[0] for group in groups]
 
     def event(g, part, step):
-        if g == -2:
+        if g == -2 and step == 3:
+            dx_swap.wait_recv()
+            unit2[0:block, :] = dx_low[1].astype(jnp.float32)
+            dx_other.start()
+        elif g == -2:
             vector_step(step)
         elif g < 0:
+            fetch("low").wait()
             out_swap.start()
+            out_keep.start()
         else:
             scatter.step(g, part, step)
+            if (g, part, step) in last:
+                result_copy(names[g]).start()
+
+    ends = {}
+    for _, g, part, step in SCATTER_EVENTS:
+        if g >= 0 and step == 3:
+            ends[names[g]] = (g, part, step)
+    last = set(ends.values())
+
+    def result_copy(name):
+        at = 4 + WEIGHTS.index(name)
+        return pltpu.make_async_copy(summed[name], grad_out[name], out_sem.at[at])
 
     clock = Clock(SCATTER_EVENTS, event, set())
 
@@ -1415,37 +1451,29 @@
         clock.begun.add(g)
         scatter.begin(g)
 
-    for name in ("unit2", "ct", "inv2", "vec", "g"):
+    for name in ("ct", "g", "vec"):
         fetch(name).start()
-    place.greet()
-
-    fetch("unit2").wait()
+    place.hail()
+
     fetch("ct").wait()
-    fetch("inv2").wait()
+    d_f = ct
     fetch("vec").wait()
-    unit = unit2[...]
-    out_low[...] = (unit * vector(G2) + vector(E2)).astype(jnp.bfloat16)
-    seed = ct[...].astype(jnp.float32)
-    vec_g[:, G2 : G2 + width] = total(seed * unit)
-    vec_g[:, E2 : E2 + width] = total(seed)
-    d_h2 = norm_back(seed, unit, inv2[:, 0:1], vector(G2))
-    unit2[...] = d_h2
-    ct[...] = d_h2.astype(jnp.bfloat16)
-    d_f = ct
-    vec_g[:, B2 : B2 + width] = total(d_f[...])
+    for n, start in enumerate((B2, G2, E2)):
+        vec_g[:, start : start + width] = vec[:, SUMS + n * width : SUMS + (n + 1) * width]
 
     def rows(at):
         return pl.ds(pl.multiple_of(at * block, block), block)
 
     out_swap = remote(out_low.at[rows(1 - y)], out_out.at[y], ex_sems, (0,), place.y_peer)
     out_keep = pltpu.make_async_copy(out_low.at[rows(y)], out_out.at[y], out_sem.at[0])
+    dx_other = pltpu.make_async_copy(unit2.at[0:block], dx_out.at[1 - y], out_sem.at[2])
     dx_swap = remote(dx_low.at[0], dx_low.at[1], ex_sems, (1,), place.y_peer)
 
     def with_down(w_down):
         fetch_weight("down", w_down).start()
         fetch("g").wait()
 
-        for name in ("d", "unit1", "inv1", "w_out", "o", "w_box", "qkv", "table"):
+        for name in ("d", "unit2", "low", "unit1", "inv1", "w_out", "o", "w_box", "qkv", "table"):
             fetch(name).start()
 
         def down_grads(first, size):
@@ -1462,6 +1490,8 @@
                 return carry
 
             lax.fori_loop(0, 4, grad_tile, 0)
+            if first == 0:
+                place.meet()
             for g, group in enumerate(groups):
                 if group[0] == "down" and first <= group[2][2] < first + size:
                     begin(g)
@@ -1469,7 +1499,6 @@
 
         down_grads(0, 128)
         down_grads(128, 256)
-        out_keep.start()
         fetch_weight("down", w_down).wait()
         fetch("d").wait()
 
@@ -1489,6 +1518,7 @@
 
     fetch("unit1").wait()
     fetch("inv1").wait()
+    fetch("unit2").wait()
     y1_low[...] = (unit1[...] * vector(G1) + vector(E1)).astype(jnp.bfloat16)
 
     def with_up(w_up):
@@ -1703,20 +1733,14 @@
         clock.point()
         clock.point()
         clock.upto(*(tuple(event) for _, *event in SCATTER_EVENTS))
-        dx_swap.wait_recv()
-        unit2[0:block, :] = dx_low[1].astype(jnp.float32)
-        pltpu.make_async_copy(unit2.at[0:block], dx_out.at[1 - y], out_sem.at[2]).start()
         for k in range(3):
             vector_z(k).wait_recv()
         piece_total = pieces[y, z, x, c]
         for k in range(3):
             piece_total = piece_total + pz_land[k]
         piece_sum[...] = piece_total
-        finals = [pltpu.make_async_copy(piece_sum, piece_out, out_sem.at[3])]
-        for i, name in enumerate(WEIGHTS):
-            finals.append(pltpu.make_async_copy(summed[name], grad_out[name], out_sem.at[4 + i]))
-        for copy in finals:
-            copy.start()
+        piece_copy = pltpu.make_async_copy(piece_sum, piece_out, out_sem.at[3])
+        piece_copy.start()
         scatter.left(range(count))
         for copy in (vector_c, vector_y, vector_x, out_swap, dx_swap):
             copy.wait_send()
@@ -1725,9 +1749,10 @@
         out_swap.wait_recv()
         out_keep.wait()
         pltpu.make_async_copy(unit1.at[rows(y)], dx_out.at[y], out_sem.at[1]).wait()
-        pltpu.make_async_copy(unit2.at[0:block], dx_out.at[1 - y], out_sem.at[2]).wait()
-        for copy in finals:
-            copy.wait()
+        dx_other.wait()
+        piece_copy.wait()
+        for name in WEIGHTS:
+            result_copy(name).wait()
 
     pl.run_scoped(
         with_qkv,
@@ -1766,9 +1791,9 @@
     scratch += [vmem(page_len, BOX_DIM)]
     scratch += [
         vmem(*kept[n].shape, kind=kept[n].dtype)
-        for n in ("o", "unit1", "inv1", "g", "d", "unit2", "inv2", "vec")
+        for n in ("o", "unit1", "inv1", "g", "d", "unit2", "low", "vec")
     ]
-    scratch += [vmem(page_len, width)] * 4
+    scratch += [vmem(page_len, width)] * 3
     scratch += [vmem(2, page_len // 2, width), vmem(1, VECTORS + 128, kind=single)]
     scratch += [
         vmem(2, 4, 2, 2, 1, 384, kind=single),

time: 169 us -> 163 us (0.964)
  Pallas kernels: 168 us -> 162 us
    pallas_call x1, Pallas kernels: 81.3 us -> 77.2 us  [backward_call(): pl.pallas_call(partial(backward_kernel, plan), out_shape=outs, in_specs=[...]
    pallas_call x1, Pallas kernels: 83.5 us -> 81.2 us  [forward_call(): pl.pallas_call(partial(forward_kernel, plan), out_shape=outs, in_specs=[a...]
where the time goes in v1:
time: 163 us
  Pallas kernels  162 us (99%)
    pallas_call x1, Pallas kernels, forward_call(): pl.pallas_call(partial(forward_kernel, plan), out_shape=outs, in_specs=[a...  81.2 us
    pallas_call x1, Pallas kernels, backward_call(): pl.pallas_call(partial(backward_kernel, plan), out_shape=outs, in_specs=[...  77.2 us
    pallas_call x1, Pallas kernels, finish_call(): pl.pallas_call(finish_kernel, out_shape=outs, grid=(2,), in_specs=halves...  3.39 us

profile of v1, /device:TPU:0, one launch (start us, length us, event | category | flops | bytes accessed | tf_op | source)
XLA Modules:
  0.0 162.7 jit_solution(4610927578969905290)
XLA Ops:
  0.6 81.2 %shard_map.161 = (bf16[2,4,2,2,48,1152]{5,4,3,2,1,0:T(8,128)(2,1)}, bf16[2,4,2,2,48,384]{5,4,3,2,1,0:T(8,128)(2,1)}, bf16[2,4,2,2,48,384]{5,4,3,2,1,0:T(8,128)(2...) custom-call(bf16[2,256,768]{2,1,0:T(8,128)(2,1)} %refs_0_.1, ...), custom_call_target="tpu_custom_call" | custom-call | tf_op jit(solution)/shard_map/pallas_call | solution.py:1170
  81.9 77.2 %shard_map.162 = (bf16[2,256,768]{2,1,0:T(8,128)(2,1)}, f32[2,256,768]{2,1,0:T(8,128)}, f32[48,1152]{1,0:T(8,128)}, f32[48,384]{1,0:T(8,128)}, f32[48,384]{1,0:T...) custom-call(bf16[2,4,2,2,48,1152]{5,4,3,2,1,0:T(8,128)(2,1)} %get-tuple-element.34.refs_0_, ...), custom_call_target="tpu_custom_call" | custom-call | tf_op jit(solution)/shard_map/pallas_call | solution.py:1812
  159.1 3.4 %shard_map.163 = (bf16[2,256,768]{2,1,0:T(8,128)(2,1)}, f32[2,256,768]{2,1,0:T(8,128)}, f32[48,1152]{1,0:T(8,128)}, f32[48,384]{1,0:T(8,128)}, f32[48,384]{1,0:T...) custom-call(bf16[2,256,768]{2,1,0:T(8,128)(2,1)} %get-tuple-element.52.refs_0_, ...), custom_call_target="tpu_custom_call" | custom-call | tf_op jit(solution)/shard_map/pallas_call | solution.py:1847
